TPU v7x, 256 devices: a whole 4x4x8 slice. The times are simulated.
256 devices in a mesh: dp: 4 (over y), seq: 16 (over z_lo, x, core), mp: 4 (over z_hi).
Axes of the slice: x: 4, y: 4, z: 8 (z_hi: 4, z_lo: 2; z = z_hi * 2 + z_lo), core: 2. Of those that a mesh axis runs over, the one named last changes fastest.
Arguments:
- queries: bfloat16 [4, 4096, 8192], P('dp', 'seq', 'mp'), may hold values from -300 to 300
- image_keys: bfloat16 [4, 16, 512, 1024], P('dp', 'seq', None, 'mp'), may hold values from -300 to 300
- image_values: bfloat16 [4, 16, 512, 1024], P('dp', 'seq', None, 'mp'), may hold values from -6 to 6
- norm_gains: float32 [2, 128], replicated, may hold values from 0.25 to 5
- image_tiles: int32 [4, 16], P('dp'), may hold values from 1 to 4, as said below
- read_mask: int32 [4, 32, 16], P('dp'), may hold values from 0 to 1, as said below
- grad_attended: bfloat16 [4, 4096, 8192], P('dp', 'seq', 'mp'), may hold values from -15 to 15
Outputs:
- attended: bfloat16 [4, 4096, 8192], P('dp', 'seq', 'mp')
- grad_queries: bfloat16 [4, 4096, 8192], P('dp', 'seq', 'mp')
- grad_keys: bfloat16 [4, 16, 512, 1024], P('dp', 'seq', None, 'mp')
- grad_values: bfloat16 [4, 16, 512, 1024], P('dp', 'seq', None, 'mp')
- grad_gains: float32 [2, 128], replicated
Inputs may be any that keep to these rules, and one draw needn't show every extreme that they name: `image_tiles`: each document has an image of 4 tiles and an image of 1 tile. `read_mask`: each text tile reads 1 to 3 images with consecutive indices; the last text tile of each document reads exactly 3.
All inputs are finite; a program needn't handle non-finite values.
Results may differ from a plain program's by a relative error of at most 0.03.
The roundings to bfloat16 on the way count: a program that leaves them out, or rounds other values in their place, can miss the bound.
Values may be sent and summed in bfloat16 or wider, within the bound.
A program may use at most 192 MiB of HBM per device.

v0:
```python
import jax
import jax.numpy as jnp
from jax import lax
from jax.sharding import PartitionSpec as P

HEAD_DIM = 128
TEXT_TILE = 128
TILE_TOK = 128
READ_MOST = 3


EPSILON = 1e-05


def read_slots(read_rows, tile_counts, slot_total):
    ranking = jnp.cumsum(read_rows, axis=1) - 1
    slot_ids = jnp.arange(slot_total, dtype=jnp.int32)
    matches = (read_rows[:, None, :] == 1) & (ranking[:, None, :] == slot_ids[None, :, None])
    match_int = matches.astype(jnp.int32)
    image_ids = jnp.arange(read_rows.shape[1], dtype=jnp.int32)
    chosen = jnp.sum(match_int * image_ids[None, None, :], axis=2)
    lengths = tile_counts * TILE_TOK
    slot_length = jnp.sum(match_int * lengths[None, None, :], axis=2)
    return (chosen, slot_length, matches)


def unit_rows(entries):
    inverse = lax.rsqrt(jnp.mean(entries * entries, axis=-1, keepdims=True) + EPSILON)
    return (entries * inverse, inverse)


def norm_backward(normed_grads, unit_part, inverse, gain_row):
    scaled = normed_grads * gain_row
    return inverse * (scaled - unit_part * jnp.mean(scaled * unit_part, axis=-1, keepdims=True))


def pick_block(tile_count, head_count):
    target = max(1, 1024 // (TEXT_TILE * head_count))
    block_size = min(tile_count, target)
    while tile_count % block_size != 0:
        block_size = block_size - 1
    return block_size


def on_device(queries, image_keys, image_values, norm_gains, image_tiles, read_mask, grad_attended):
    seq_index = lax.axis_index("seq")
    owner_keys = image_keys[0, 0]
    max_tokens = owner_keys.shape[0]
    kv_width = owner_keys.shape[1]
    kv_local = kv_width // HEAD_DIM
    score_scale = HEAD_DIM ** (-0.5)
    query_rows = queries[0]
    token_total = query_rows.shape[0]
    head_width = query_rows.shape[1]
    group_count = head_width // kv_width
    key_all, value_all = (
        lax.all_gather(image_keys[0], "seq", axis=0, tiled=True),
        lax.all_gather(image_values[0], "seq", axis=0, tiled=True),
    )
    image_total = key_all.shape[0]
    key_source = key_all.reshape(image_total, max_tokens, kv_local, HEAD_DIM)
    value_source = value_all.reshape(image_total, max_tokens, kv_local, HEAD_DIM)
    tiles_here = token_total // TEXT_TILE
    mask_rows = lax.dynamic_slice_in_dim(read_mask[0], seq_index * tiles_here, tiles_here, 0)
    image_count = key_source.shape[0]
    slot_total = min(READ_MOST, image_count)
    chosen, slot_length, matches = read_slots(mask_rows, image_tiles[0], slot_total)
    tile_total = token_total // TEXT_TILE
    block_tiles = pick_block(tile_total, group_count * kv_local)
    block_total = tile_total // block_tiles
    slot_width = slot_total * max_tokens
    query_groups = query_rows.reshape(token_total, kv_local, group_count, HEAD_DIM)
    query_unit, query_inverse = unit_rows(query_groups.astype(jnp.float32))
    query_normed = (query_unit * norm_gains[0]).astype(jnp.bfloat16)
    key_unit_here, unused_inverse = unit_rows(key_source.astype(jnp.float32))
    key_normed = (key_unit_here * norm_gains[1]).astype(jnp.bfloat16)
    chosen_blocks = chosen.reshape(block_total, block_tiles, slot_total)
    length_blocks = slot_length.reshape(block_total, block_tiles, slot_total)
    match_blocks = matches.astype(jnp.float32).reshape(
        block_total, block_tiles, slot_total, image_count
    )
    key_index = jnp.arange(max_tokens, dtype=jnp.int32)

    def slot_rows(source, chosen_block):
        return source[chosen_block].reshape(block_tiles, slot_width, kv_local, HEAD_DIM)

    def block_weights(query_block, key_rows, length_block):
        allowed = (key_index[None, None, :] < length_block[:, :, None]).reshape(
            block_tiles, 1, 1, 1, slot_width
        )
        scores = (
            jnp.einsum(
                "tqegd,tked->tegqk", query_block, key_rows, preferred_element_type=jnp.float32
            )
            * score_scale
        )
        masked = jnp.where(allowed, scores, -1e30)
        row_peak = jnp.max(masked, axis=4, keepdims=True)
        exponent = jnp.where(allowed, jnp.exp(masked - row_peak), 0.0)
        return (exponent / jnp.sum(exponent, axis=4, keepdims=True)).astype(jnp.bfloat16)

    def to_tiles(group_rows):
        return group_rows.reshape(
            block_total, block_tiles, TEXT_TILE, kv_local, group_count, HEAD_DIM
        )

    def forward_block(block_items):
        query_block, chosen_block, length_block = block_items
        key_rows = slot_rows(key_normed, chosen_block)
        value_rows = slot_rows(value_source, chosen_block)
        weights = block_weights(query_block, key_rows, length_block)
        return jnp.einsum(
            "tegqk,tked->tqegd", weights, value_rows, preferred_element_type=jnp.float32
        ).astype(jnp.bfloat16)

    output_blocks = lax.map(forward_block, (to_tiles(query_normed), chosen_blocks, length_blocks))
    output_rows = output_blocks.reshape(token_total, head_width)
    cotangent_rows = grad_attended[0]
    cotangent_groups = cotangent_rows.reshape(token_total, kv_local, group_count, HEAD_DIM)

    def backward_block(carried, block_items):
        key_total, value_total = carried
        query_block, cotangent_block, chosen_block, length_block, match_block = block_items
        key_rows = slot_rows(key_normed, chosen_block)
        value_rows = slot_rows(value_source, chosen_block)
        weights = block_weights(query_block, key_rows, length_block)
        weight_values = weights.astype(jnp.float32)
        value_scores = jnp.einsum(
            "tqegd,tked->tegqk", cotangent_block, value_rows, preferred_element_type=jnp.float32
        )
        row_dot = jnp.sum(weight_values * value_scores, axis=4, keepdims=True)
        score_grads = (weight_values * (value_scores - row_dot)).astype(jnp.bfloat16)
        query_grads = (
            jnp.einsum(
                "tegqk,tked->tqegd", score_grads, key_rows, preferred_element_type=jnp.float32
            )
            * score_scale
        )
        key_slots = (
            jnp.einsum(
                "tegqk,tqegd->tked", score_grads, query_block, preferred_element_type=jnp.float32
            )
            * score_scale
        )
        value_slots = jnp.einsum(
            "tegqk,tqegd->tked", weights, cotangent_block, preferred_element_type=jnp.float32
        )
        key_slots = key_slots.reshape(block_tiles, slot_total, max_tokens, kv_local, HEAD_DIM)
        value_slots = value_slots.reshape(block_tiles, slot_total, max_tokens, kv_local, HEAD_DIM)
        key_total = key_total + jnp.einsum("tri,trked->iked", match_block, key_slots)
        value_total = value_total + jnp.einsum("tri,trked->iked", match_block, value_slots)
        return ((key_total, value_total), query_grads)

    zero_grads = jnp.zeros((image_count, max_tokens, kv_local, HEAD_DIM), jnp.float32)
    (key_totals, value_totals), query_grad_blocks = lax.scan(
        backward_block,
        (zero_grads, zero_grads),
        (
            to_tiles(query_normed),
            to_tiles(cotangent_groups),
            chosen_blocks,
            length_blocks,
            match_blocks,
        ),
    )
    query_grads = query_grad_blocks.reshape(token_total, kv_local, group_count, HEAD_DIM)
    grad_query_groups = norm_backward(query_grads, query_unit, query_inverse, norm_gains[0]).astype(
        jnp.bfloat16
    )
    grad_query_rows = grad_query_groups.reshape(token_total, head_width)
    query_gain = jnp.sum(query_grads * query_unit, axis=(0, 1, 2))
    key_parts, value_parts = (
        lax.psum_scatter(key_totals, "seq", scatter_dimension=0, tiled=True),
        lax.psum_scatter(value_totals, "seq", scatter_dimension=0, tiled=True),
    )
    key_grads = key_parts.reshape(max_tokens, kv_local, HEAD_DIM)
    value_grads = value_parts.reshape(max_tokens, kv_local, HEAD_DIM)
    owner_heads = owner_keys.astype(jnp.float32).reshape(max_tokens, kv_local, HEAD_DIM)
    key_unit, key_inverse = unit_rows(owner_heads)
    grad_key_rows = (
        norm_backward(key_grads, key_unit, key_inverse, norm_gains[1])
        .astype(jnp.bfloat16)
        .reshape(max_tokens, kv_width)
    )
    grad_value_rows = value_grads.astype(jnp.bfloat16).reshape(max_tokens, kv_width)
    key_gain = jnp.sum(key_grads * key_unit, axis=(0, 1))
    grad_gains = lax.psum(jnp.stack([query_gain, key_gain]), ("dp", "seq", "mp"))
    return (
        output_rows[None],
        grad_query_rows[None],
        grad_key_rows[None, None],
        grad_value_rows[None, None],
        grad_gains,
    )


def solution(mesh):
    in_specs = (
        P("dp", "seq", "mp"),
        P("dp", "seq", None, "mp"),
        P("dp", "seq", None, "mp"),
        P(),
        P("dp", None),
        P("dp", None, None),
        P("dp", "seq", "mp"),
    )
    out_specs = (
        P("dp", "seq", "mp"),
        P("dp", "seq", "mp"),
        P("dp", "seq", None, "mp"),
        P("dp", "seq", None, "mp"),
        P(),
    )
    return jax.shard_map(
        on_device, mesh=mesh, in_specs=in_specs, out_specs=out_specs, check_vma=False
    )
```

profile of v0, /device:TPU:1, one launch (start us, length us, event | category | flops | bytes accessed | tf_op | source)
XLA Modules:
  0.0 438.6 jit_solution(7596800300522395899)
XLA Ops:
  21.7 32.4 %all-gather.7.cloned.1.call-done = bf16[16,1,512,256]{3,2,1,0:T(8,128)(2,1)} async-done(((bf16[1,1,512,256]{3,2,1,0:T(8,128)(2,1)}), bf16[16,1,512,256]{3,2,1,0:T(8,128)(2,1)}) %all-gather.7.cloned.1.call-update) | async-done | bytes 4194320 | tf_op jit(solution)/shard_map/all_gather | solution.py:57
  54.2 9.0 %reshape.501 = f32[16,512,2,128]{3,2,1,0:T(2,128)} reshape(bf16[16,1,512,256]{3,2,1,0:T(8,128)(2,1)} %all-gather.7.cloned.1.call-done) | data formatting | bytes 12582912 | tf_op jit(solution)/shard_map/convert_element_type | solution.py:75
  63.2 13.0 %multiply_reduce_fusion = f32[16,512,2]{2,1,0:T(8,128)} fusion(f32[16,512,2,128]{3,2,1,0:T(2,128)} %reshape.501), kind=kLoop, calls=%fused_computation.87 | loop fusion | flops 4177920 | bytes 8454144 | tf_op jit(solution)/shard_map/reduce_sum | solution.py:28
  81.8 13.1 %multiply_convert_fusion = bf16[16,512,2,128]{3,2,1,0:T(2,128)(2,1)} fusion(f32[16,512,2,128]{3,2,1,0:T(2,128)} %reshape.501, f32[128]{0:T(128)S(1)} %get-tuple-element.379, f32[16,512,2]{2,1,0:T(8,128)} %copy.233), kind=kLoop, calls=%fused_computation.86 | loop fusion | flops 6291456 | bytes 12648960 | tf_op jit(solution)/shard_map/convert_element_type | solution.py:76
  96.0 7.0 %reshape.496 = bf16[16,512,2,128]{3,2,1,0:T(2,128)(2,1)} reshape(bf16[16,1,512,256]{3,2,1,0:T(8,128)(2,1)} %all-gather.5.cloned.1.call-done) | data formatting | bytes 8388608 | tf_op jit(solution)/shard_map/reshape | solution.py:62
  103.0 133.5 %while.27 = (s32[]{:T(128)}, f32[16,512,2,128]{3,0,2,1:T(8,128)}, f32[16,512,2,128]{3,0,2,1:T(8,128)}, f32[2,1,128,2,8,128]{2,5,4,3,1,0:T(8,128)}, bf16[2,1,3,16...) while((s32[]{:T(128)}, f32[16,512,2,128]{3,0,2,1:T(8,128)}, ...), condition=%wide.region_13.14_spmd.clone, body=%wide.region_9.13_spmd.clone.sunk | while | flops 4127191552 | bytes 290314176 | solution.py:155
  120.7 5.3 %gather_fusion.3 = bf16[3,512,2,128]{3,2,1,0:T(2,128)(2,1)} fusion(bf16[16,512,2,128]{3,2,1,0:T(2,128)(2,1)} %get-tuple-element.563, s32[1024]{0:T(1024)S(1)} %pad_clamp_fusion.5), kind=kCustom, calls=%fused_computation.3.clone.clone.1 | custom fusion | bytes 1572876 | tf_op jit(solution)/shard_map/while/body/eval_jaxpr/gather | solution.py:85
  127.1 8.6 %fusion.123 = (f32[2,8,128]{2,1,0:T(8,128)S(1)}, bf16[1,2,8,128,1536]{3,4,2,1,0:T(8,128)(2,1)S(1)}, f32[2,1536,128,8]{2,1,3,0:T(8,128)S(1)}) fusion(f32[2,8,128]{2,1,0:T(8,128)S(1)} %fusion.122, f32[2,8,128]{2,1,0:T(8,128)S(1)} %get-tuple-element.500, f32[2,1536,128,8]{2,1,3,0:T(8,128)} %copy-done.3, pred[1536]{0:T(1024)(128)(4,1)S(1)} %lt.131, ...), kind=kOutput, calls=%fused_computation.37.clone.1 | convolution fusion | flops 833615872 | bytes 32794112 | tf_op jit(solution)/shard_map/while/body/eval_jaxpr/tqegd,tked->tegqk/dot_general | solution.py:128
  147.4 6.1 %select_add_fusion.4 = f32[16,512,2,128]{3,0,2,1:T(8,128)} fusion(f32[16,512,2,128]{3,0,2,1:T(8,128)} %get-tuple-element.542, pred[]{:T(512)S(6)} %compare.3, bf16[3,512,2,128]{3,1,0,2:T(8,128)(2,1)} %bitcast.350, bf16[2,1,3,16]{3,2,1,0:T(4,128)(2,1)S(1)} %get-tuple-element.558, s32[]{:T(128)} %get-tuple-element.541), kind=kOutput, calls=%fused_computation.48.clone.1 | convolution fusion | flops 16777216 | bytes 17564676 | tf_op jit(solution)/shard_map/while/body/eval_jaxpr/tri,trked->iked/dot_general | solution.py:150
  159.1 6.0 %select_add_fusion.5 = f32[16,512,2,128]{3,0,2,1:T(8,128)} fusion(f32[16,512,2,128]{3,0,2,1:T(8,128)} %get-tuple-element.543, pred[]{:T(512)S(6)} %compare.3, bf16[3,512,2,128]{3,1,0,2:T(8,128)(2,1)} %bitcast.351, bf16[2,1,3,16]{3,2,1,0:T(4,128)(2,1)S(1)} %get-tuple-element.558, s32[]{:T(128)} %get-tuple-element.541), kind=kOutput, calls=%fused_computation.47.clone.1 | convolution fusion | flops 16777216 | bytes 17564676 | tf_op jit(solution)/shard_map/while/body/eval_jaxpr/tri,trked->iked/dot_general | solution.py:151
  184.7 5.3 %gather_fusion.3 = bf16[3,512,2,128]{3,2,1,0:T(2,128)(2,1)} fusion(bf16[16,512,2,128]{3,2,1,0:T(2,128)(2,1)} %get-tuple-element.563, s32[1024]{0:T(1024)S(1)} %pad_clamp_fusion.5), kind=kCustom, calls=%fused_computation.3.clone.clone.1 | custom fusion | bytes 1572876 | tf_op jit(solution)/shard_map/while/body/eval_jaxpr/gather | solution.py:85
  191.1 8.6 %fusion.123 = (f32[2,8,128]{2,1,0:T(8,128)S(1)}, bf16[1,2,8,128,1536]{3,4,2,1,0:T(8,128)(2,1)S(1)}, f32[2,1536,128,8]{2,1,3,0:T(8,128)S(1)}) fusion(f32[2,8,128]{2,1,0:T(8,128)S(1)} %fusion.122, f32[2,8,128]{2,1,0:T(8,128)S(1)} %get-tuple-element.500, f32[2,1536,128,8]{2,1,3,0:T(8,128)} %copy-done.3, pred[1536]{0:T(1024)(128)(4,1)S(1)} %lt.131, ...), kind=kOutput, calls=%fused_computation.37.clone.1 | convolution fusion | flops 833615872 | bytes 32794112 | tf_op jit(solution)/shard_map/while/body/eval_jaxpr/tqegd,tked->tegqk/dot_general | solution.py:128
  211.5 8.6 %select_add_fusion.4 = f32[16,512,2,128]{3,0,2,1:T(8,128)} fusion(f32[16,512,2,128]{3,0,2,1:T(8,128)} %get-tuple-element.542, pred[]{:T(512)S(6)} %compare.3, bf16[3,512,2,128]{3,1,0,2:T(8,128)(2,1)} %bitcast.350, bf16[2,1,3,16]{3,2,1,0:T(4,128)(2,1)S(1)} %get-tuple-element.558, s32[]{:T(128)} %get-tuple-element.541), kind=kOutput, calls=%fused_computation.48.clone.1 | convolution fusion | flops 16777216 | bytes 17564676 | tf_op jit(solution)/shard_map/while/body/eval_jaxpr/tri,trked->iked/dot_general | solution.py:150
  225.6 8.5 %select_add_fusion.5 = f32[16,512,2,128]{3,0,2,1:T(8,128)} fusion(f32[16,512,2,128]{3,0,2,1:T(8,128)} %get-tuple-element.543, pred[]{:T(512)S(6)} %compare.3, bf16[3,512,2,128]{3,1,0,2:T(8,128)(2,1)} %bitcast.351, bf16[2,1,3,16]{3,2,1,0:T(4,128)(2,1)S(1)} %get-tuple-element.558, s32[]{:T(128)} %get-tuple-element.541), kind=kOutput, calls=%fused_computation.47.clone.1 | convolution fusion | flops 16777216 | bytes 17564676 | tf_op jit(solution)/shard_map/while/body/eval_jaxpr/tri,trked->iked/dot_general | solution.py:151
  236.4 11.6 %copy.250 = f32[16,512,2,128]{3,1,2,0:T(8,128)} copy(f32[16,512,2,128]{3,0,2,1:T(8,128)} %get-tuple-element.113) | data formatting | bytes 16777216 | tf_op jit(solution)/shard_map/while | solution.py:155
  248.1 10.0 %copy.253 = f32[16,512,2,128]{1,3,2,0:T(8,128)} copy(f32[16,512,2,128]{3,0,2,1:T(8,128)} %get-tuple-element.114) | data formatting | bytes 16777216 | tf_op jit(solution)/shard_map/while | solution.py:155
  277.7 60.4 %while.26 = (s32[]{:T(128)}, bf16[2,1,128,2,8,128]{5,4,3,2,0,1:T(8,128)(2,1)}, s32[2,1,3]{2,1,0:T(1,128)S(1)}, bf16[16,512,2,128]{3,2,1,0:T(2,128)(2,1)}, s32[2,...) while((s32[]{:T(128)}, ...), condition=%wide.region_8.9_spmd.clone, body=%wide.region_5.8_spmd.clone.sunk | while | flops 1654913536 | bytes 104434448 | solution.py:116
  277.7 4.5 %gather_fusion = bf16[3,512,2,128]{3,2,1,0:T(2,128)(2,1)S(1)} fusion(bf16[16,512,2,128]{3,2,1,0:T(2,128)(2,1)} %get-tuple-element.525, s32[1024]{0:T(1024)S(1)} %pad_clamp_fusion.4), kind=kCustom, calls=%fused_computation.1.clone.clone.1 | custom fusion | bytes 1572876 | tf_op jit(solution)/shard_map/while/body/eval_jaxpr/gather | solution.py:85
  285.5 4.5 %copy-done.4 = f32[2,1536,128,8]{2,1,3,0:T(8,128)} copy-done((f32[2,1536,128,8]{2,1,3,0:T(8,128)}, f32[2,1536,128,8]{2,1,3,0:T(8,128)S(1)}, u32[]{:S(2)}) %copy-start.4) | copy-done | bytes 12582936 | tf_op jit(solution)/shard_map/while
  298.2 8.2 %fusion.109 = bf16[1,1,128,2,8,128]{2,5,4,3,1,0:T(8,128)(2,1)S(1)} fusion(f32[2,8,128]{2,1,0:T(8,128)S(1)} %fusion.108, f32[2,8,128]{2,1,0:T(8,128)S(1)} %get-tuple-element.487, f32[2,1536,128,8]{2,1,3,0:T(8,128)} %copy-done.4, pred[1536]{0:T(1024)(128)(4,1)S(1)} %lt.126, bf16[1536,2,128,1]{2,1,0,3:T(2,128)(2,1)S(1)} %bitcast.355), kind=kOutput, calls=%fused_computation.16.clone.1 | convolution fusion | flops 824442880 | bytes 13911552 | tf_op jit(solution)/shard_map/while/body/eval_jaxpr/tegqk,tked->tqegd/dot_general | solution.py:112
  315.6 4.5 %copy-done.4 = f32[2,1536,128,8]{2,1,3,0:T(8,128)} copy-done((f32[2,1536,128,8]{2,1,3,0:T(8,128)}, f32[2,1536,128,8]{2,1,3,0:T(8,128)S(1)}, u32[]{:S(2)}) %copy-start.4) | copy-done | bytes 12582936 | tf_op jit(solution)/shard_map/while
  328.3 8.1 %fusion.109 = bf16[1,1,128,2,8,128]{2,5,4,3,1,0:T(8,128)(2,1)S(1)} fusion(f32[2,8,128]{2,1,0:T(8,128)S(1)} %fusion.108, f32[2,8,128]{2,1,0:T(8,128)S(1)} %get-tuple-element.487, f32[2,1536,128,8]{2,1,3,0:T(8,128)} %copy-done.4, pred[1536]{0:T(1024)(128)(4,1)S(1)} %lt.126, bf16[1536,2,128,1]{2,1,0,3:T(2,128)(2,1)S(1)} %bitcast.355), kind=kOutput, calls=%fused_computation.16.clone.1 | convolution fusion | flops 824442880 | bytes 13911552 | tf_op jit(solution)/shard_map/while/body/eval_jaxpr/tegqk,tked->tqegd/dot_general | solution.py:112
  340.5 4.8 %fusion.66 = bf16[1,256,2048]{2,1,0:T(8,128)(2,1)} fusion(f32[1,256,2048]{2,1,0:T(8,128)} %mul.278, f32[1,256,2048]{2,1,0:T(8,128)} %mul.287, bf16[1,256,2048]{2,1,0:T(8,128)(2,1)S(1)} %copy-done.9, f32[1,256,2048]{2,1,0:T(8,128)} %reshape.498, f32[2048]{0:T(1024)S(1)} %copy-done.20), kind=kLoop, calls=%fused_computation.95 | loop fusion | flops 3670016 | bytes 8396800 | tf_op jit(solution)/shard_map/convert_element_type | solution.py:167
  347.9 82.0 %psum.7 = f32[2,128]{1,0:T(2,128)} all-reduce(f32[2,128]{1,0:T(2,128)S(1)} %pad_maximum_fusion), channel_id=1, replica_groups=mesh['dp'=4,'seq'=16,'mp'=4] {'dp','seq','mp'}, use_global_device_ids=true, to_apply=%region_21.22 | all-reduce | flops 256 | bytes 2048 | tf_op jit(solution)/shard_map/psum | solution.py:187
  (220 shorter events, 153.3 us)
Async XLA Ops:
  7.2 47.0 %all-gather.7.cloned.1.call-start = ((), (), s32[]{:S(2)}) async-start(), calls=%async_computation.5 | async-start | bytes 4456448 | tf_op jit(solution)/shard_map/all_gather | solution.py:57
  7.9 88.1 %all-gather.5.cloned.1.call-start = ((), (), s32[]{:S(2)}) async-start(), calls=%async_computation.4 | async-start | bytes 4456448 | tf_op jit(solution)/shard_map/all_gather | solution.py:58
  8.7 336.6 %reduce-scatter.3.cloned.1.call-start = ((), (), s32[]{:S(2)}) async-start(), calls=%async_computation.2 | async-start | bytes 8912896 | tf_op jit(solution)/shard_map/reduce_scatter | solution.py:173
  17.6 45.6 %copy-start.6 = (f32[2,1,128,2,8,128]{2,5,4,3,1,0:T(8,128)}, f32[2,1,128,2,8,128]{2,5,4,3,1,0:T(8,128)S(1)}, u32[]{:S(2)}) copy-start(f32[2,1,128,2,8,128]{2,5,4,3,1,0:T(8,128)S(1)} %copy.236) | copy-start | bytes 6291460
  17.6 45.6 %copy-start.21 = (f32[128]{0:T(128)}, f32[128]{0:T(128)S(1)}, u32[]{:S(2)}) copy-start(f32[128]{0:T(128)S(1)} %get-tuple-element.378) | copy-start | bytes 1540
  17.6 64.2 %copy-start.23 = (f32[128]{0:T(128)}, f32[128]{0:T(128)S(1)}, u32[]{:S(2)}) copy-start(f32[128]{0:T(128)S(1)} %get-tuple-element.379) | copy-start | bytes 1540
  145.0 8.5 %slice-start.2 = ((s8[6291456]{0:T(1024)(128)(4,1)}), s8[2097152]{0:T(1024)(128)(4,1)S(1)}, s32[]{:S(2)}) async-start(s8[6291456]{0:T(1024)(128)(4,1)} %bitcast.348), calls=%async_computation.8 | async-start | bytes 4194304 | tf_op jit(solution)/shard_map/while
  209.0 11.0 %slice-start.2 = ((s8[6291456]{0:T(1024)(128)(4,1)}), s8[2097152]{0:T(1024)(128)(4,1)S(1)}, s32[]{:S(2)}) async-start(s8[6291456]{0:T(1024)(128)(4,1)} %bitcast.348), calls=%async_computation.8 | async-start | bytes 4194304 | tf_op jit(solution)/shard_map/while
  211.5 8.6 %slice-start.3 = ((s8[6291456]{0:T(1024)(128)(4,1)}), s8[4194304]{0:T(1024)(128)(4,1)S(1)}, s32[]{:S(2)}) async-start(s8[6291456]{0:T(1024)(128)(4,1)} %bitcast.348), calls=%async_computation.9 | async-start | bytes 8388608 | tf_op jit(solution)/shard_map/while
  223.1 11.0 %slice-start = ((s8[6291456]{0:T(1024)(128)(4,1)}), s8[2097152]{0:T(1024)(128)(4,1)S(1)}, s32[]{:S(2)}) async-start(s8[6291456]{0:T(1024)(128)(4,1)} %bitcast.346), calls=%async_computation.6 | async-start | bytes 4194304 | tf_op jit(solution)/shard_map/while
  225.6 8.5 %slice-start.1 = ((s8[6291456]{0:T(1024)(128)(4,1)}), s8[4194304]{0:T(1024)(128)(4,1)S(1)}, s32[]{:S(2)}) async-start(s8[6291456]{0:T(1024)(128)(4,1)} %bitcast.346), calls=%async_computation.7 | async-start | bytes 8388608 | tf_op jit(solution)/shard_map/while
  248.0 181.9 %reduce-scatter.5.cloned.1.call-start = ((), (), s32[]{:S(2)}) async-start(), calls=%async_computation.3 | async-start | bytes 8912896 | tf_op jit(solution)/shard_map/reduce_scatter | solution.py:174
  258.1 11.6 %copy-start.7 = (f32[2,1,128,2,8,128]{2,5,4,3,1,0:T(8,128)S(1)}, f32[2,1,128,2,8,128]{2,5,4,3,1,0:T(8,128)}, u32[]{:S(2)}) copy-start(f32[2,1,128,2,8,128]{2,5,4,3,1,0:T(8,128)} %copy-done.6) | copy-start | bytes 6291460
  258.1 11.6 %copy-start.17 = (f32[2,1,2,8,128]{4,3,1,0,2:T(8,128)S(1)}, f32[2,1,2,8,128]{4,3,1,0,2:T(8,128)}, u32[]{:S(2)}) copy-start(f32[2,1,2,8,128]{4,3,1,0,2:T(8,128)} %copy-done.16) | copy-start | bytes 49156
  259.2 14.2 %copy-start.10 = (bf16[1,1,512,256]{2,3,1,0:T(8,128)(2,1)}, bf16[1,1,512,256]{2,3,1,0:T(8,128)(2,1)S(1)}, u32[]{:S(2)}) copy-start(bf16[1,1,512,256]{2,3,1,0:T(8,128)(2,1)S(1)} %copy.249) | copy-start | bytes 786436
  277.7 62.8 %copy-start.9 = (bf16[1,256,2048]{2,1,0:T(8,128)(2,1)S(1)}, bf16[1,256,2048]{2,1,0:T(8,128)(2,1)}, u32[]{:S(2)}) copy-start(bf16[1,256,2048]{2,1,0:T(8,128)(2,1)} %param.11) | copy-start | bytes 3145732
  277.7 62.8 %copy-start.20 = (f32[2048]{0:T(1024)S(1)}, f32[2048]{0:T(1024)}, u32[]{:S(2)}) copy-start(f32[2048]{0:T(1024)} %broadcast_bitcast_fusion) | copy-start | bytes 24580
  298.2 8.7 %copy-start.13 = (bf16[2,1,128,2,8,128]{5,4,3,2,0,1:T(8,128)(2,1)S(1)}, bf16[2,1,128,2,8,128]{5,4,3,2,0,1:T(8,128)(2,1)}, u32[]{:S(2)}) copy-start(bf16[2,1,128,2,8,128]{5,4,3,2,0,1:T(8,128)(2,1)} %get-tuple-element.513) | copy-start | bytes 3145732 | tf_op jit(solution)/shard_map/while
  328.3 8.6 %copy-start.13 = (bf16[2,1,128,2,8,128]{5,4,3,2,0,1:T(8,128)(2,1)S(1)}, bf16[2,1,128,2,8,128]{5,4,3,2,0,1:T(8,128)(2,1)}, u32[]{:S(2)}) copy-start(bf16[2,1,128,2,8,128]{5,4,3,2,0,1:T(8,128)(2,1)} %get-tuple-element.513) | copy-start | bytes 3145732 | tf_op jit(solution)/shard_map/while
  338.1 8.5 %copy-start.12 = (f32[512,2,128]{0,2,1:T(8,128)S(1)}, f32[512,2,128]{0,2,1:T(8,128)}, u32[]{:S(2)}) copy-start(f32[512,2,128]{0,2,1:T(8,128)} %get-tuple-element.370) | copy-start | bytes 1572868
  338.1 8.8 %copy-start.11 = (bf16[1,1,512,256]{2,3,1,0:T(8,128)(2,1)S(1)}, bf16[1,1,512,256]{2,3,1,0:T(8,128)(2,1)}, u32[]{:S(2)}) copy-start(bf16[1,1,512,256]{2,3,1,0:T(8,128)(2,1)} %copy-done.10) | copy-start | bytes 786436
  338.1 8.8 %copy-start.27 = (f32[256]{0:T(256)S(1)}, f32[256]{0:T(256)}, u32[]{:S(2)}) copy-start(f32[256]{0:T(256)} %broadcast_bitcast_fusion.1) | copy-start | bytes 3076
  338.1 9.8 %copy-start.26 = (f32[128]{0:T(128)S(1)}, f32[128]{0:T(128)}, u32[]{:S(2)}) copy-start(f32[128]{0:T(128)} %get-tuple-element.325) | copy-start | bytes 1540
  338.1 93.7 %copy-start.1 = (s32[1,32,16]{1,2,0:T(8,128)S(1)}, s32[1,32,16]{1,2,0:T(8,128)}, u32[]{:S(2)}) copy-start(s32[1,32,16]{1,2,0:T(8,128)} %param.16) | copy-start | bytes 6148
  (23 other events, 103.4 us)
Sparse Core Ops, SparseCore 0:
  9.9 44.2 all-gather.6
  56.0 39.9 all-gather.4
  248.2 72.8 reduce-scatter.2
  323.5 76.0 reduce-scatter.4
where the time goes:
time: 446 us; the launch traced here: 439 us
  local copies, waits for them, and re-layouts  150 us (34%)
  matrix products  95.5 us (21%)
  blocking collectives  82 us (18%)
  other arithmetic  60.6 us (14%)
  waiting for transfers between devices  34.9 us (8%)
  between operations  14.4 us (3%)
    psum x1, blocking collectives, on_device(): lax.psum(jnp.stack([query_gain, key_gain]), ('dp', 'seq', 'mp'))  82 us
    gather x8, local copies, waits for them, and re-layouts, slot_rows(): source[chosen_block].reshape(block_tiles, slot_width, kv_local, HEAD_DIM)  37 us
    all_gather x1, waiting for transfers between devices, on_device(): lax.all_gather(image_keys[0], 'seq', axis=0, tiled=True)  32.4 us
    while x40, local copies, waits for them, and re-layouts  26.3 us
    while x3, local copies, waits for them, and re-layouts, on_device(): lax.scan(backward_block, (zero_grads, zero_grads), (to_tiles(query_normed...  24.6 us
    dot_general x2, matrix products, backward_block(): jnp.einsum('tqegd,tked->tegqk', cotangent_block, value_rows, preferred_el...  17.2 us
    dot_general x2, matrix products, forward_block(): jnp.einsum('tegqk,tked->tqegd', weights, value_rows, preferred_element_ty...  16.3 us
    reduce_sum x4, other arithmetic, block_weights(): jnp.sum(exponent, axis=4, keepdims=True)  15.3 us
  transfers between devices with their start and end apart: 4, of which 2 were waited for; matrix products, arithmetic and copies ran while one was open for 32% of the time, Pallas kernels for 0%

commit v1 on v0

v1 whole, which is shorter than its diff:
```python
import functools

import jax
import jax.numpy as jnp
from jax import lax
from jax.experimental import pallas as pl
from jax.experimental.pallas import tpu as pltpu
from jax.sharding import PartitionSpec as P

HEAD_DIM = 128
TEXT_TILE = 128
TILE_TOK = 128
READ_MOST = 3
EPSILON = 1e-05
LOG2E = 1.4426950408889634
MESH = pl.DeviceIdType.MESH
BF16 = jnp.bfloat16
F32 = jnp.float32

RING = 4


def dot(a, b):
    return jnp.dot(a, b, preferred_element_type=F32)


def kernel(
    images,
    group,
    q_ref,
    do_ref,
    k_ref,
    v_ref,
    gains_ref,
    tiles_ref,
    mask_ref,
    o_out,
    dq_out,
    dk_out,
    dv_out,
    gain_out,
    q4,
    do4,
    kraw,
    kbuf,
    vbuf,
    qn,
    qnt,
    dot_t,
    don,
    ut,
    rinv,
    wbuf,
    sbuf,
    vslot,
    kslot,
    vsend,
    ksend,
    vland,
    kland,
    obuf,
    dqbuf,
    gkbuf,
    gvbuf,
    qgain,
    gcol,
    local_sem,
    swap_send,
    swap_recv,
    ag_send,
    ag_recv,
    rs_send,
    rs_recv,
    out_local,
    out_send,
    out_recv,
):
    max_tokens = k_ref.shape[0]
    tokens = q_ref.shape[0]
    half = group * HEAD_DIM
    pair_width = 2 * HEAD_DIM
    pairs = group // 2
    tile_total = 2 * tokens // TEXT_TILE
    subs = max_tokens // TILE_TOK
    scale = HEAD_DIM ** (-0.5)

    seq = lax.axis_index("seq")
    core = lax.rem(seq, 2)
    x = lax.rem(lax.div(seq, 2), RING)
    z = lax.div(seq, 2 * RING)
    other = 1 - core

    def image_at(zz, xx, parity):
        return zz * (2 * RING) + lax.rem(xx + RING, RING) * 2 + parity

    peer = image_at(z, x, other)
    right = image_at(z, x + 1, core)
    left = image_at(z, x - 1, core)
    across = image_at(1 - z, x, core)
    chip = image_at(z, x, 0)

    def columns(index, width):
        return pl.ds(pl.multiple_of(index * width, width), width)

    own_rows = columns(core, tokens)
    other_rows = columns(other, tokens)

    def remote(src, dst, send_sem, recv_sem, device):
        return pltpu.make_async_remote_copy(
            src_ref=src,
            dst_ref=dst,
            send_sem=send_sem,
            recv_sem=recv_sem,
            device_id={"seq": device},
            device_id_type=MESH,
        )

    mine = [
        pltpu.make_async_copy(k_ref.at[:, columns(core, HEAD_DIM)], kraw.at[core], local_sem.at[0]),
        pltpu.make_async_copy(
            v_ref.at[:, columns(core, HEAD_DIM)], vbuf.at[chip + core], local_sem.at[1]
        ),
        pltpu.make_async_copy(q_ref.at[:, columns(core, half)], q4.at[own_rows], local_sem.at[2]),
        pltpu.make_async_copy(do_ref.at[:, columns(core, half)], do4.at[own_rows], local_sem.at[3]),
    ]
    for copy in mine:
        copy.start()

    barrier = pltpu.get_barrier_semaphore()
    for device in (peer, right, left, across):
        pl.semaphore_signal(barrier, inc=1, device_id={"seq": device}, device_id_type=MESH)
    pl.semaphore_wait(barrier, 4)

    swaps = [
        (k_ref.at[:, columns(other, HEAD_DIM)], kraw.at[core]),
        (v_ref.at[:, columns(other, HEAD_DIM)], vbuf.at[chip + core]),
        (q_ref.at[:, columns(other, half)], q4.at[own_rows]),
        (do_ref.at[:, columns(other, half)], do4.at[own_rows]),
    ]
    swaps = [
        remote(src, dst, swap_send.at[i], swap_recv.at[i], peer)
        for i, (src, dst) in enumerate(swaps)
    ]
    for copy in swaps:
        copy.start()

    tile_base = lax.div(seq, 2) * tile_total
    first, count = [], []
    for t in range(tile_total):
        begin = jnp.int32(images)
        total = jnp.int32(0)
        for i in range(images):
            flag = mask_ref[tile_base + t, i]
            total = total + flag
            begin = jnp.where((flag == 1) & (begin == images), i, begin)
        first.append(begin)
        count.append(total)

    def pick(values, t):
        out = values[0]
        for k in range(1, len(values)):
            out = jnp.where(t == k, values[k], out)
        return out

    def reads(t):
        begin = pick(first, t)
        total = pick(count, t)
        found = []
        for r in range(READ_MOST):
            image = jnp.minimum(begin + r, images - 1)
            length = jnp.where(r < total, tiles_ref[image] * TILE_TOK, 0)
            found.append((image, length))
        return found

    def gather_copy(buf, which, number, parity):
        if number == 6:
            image, device = image_at(z, x, parity), right
        elif number == 7:
            image, device = image_at(z, x, parity), left
        elif number == 4:
            image, device = image_at(z, x, parity), across
        elif number == 5 and parity == 0:
            image, device = image_at(z, x - 1, 0), right
        elif number == 5:
            image, device = image_at(z, x + 1, 1), left
        elif number == 1:
            image, device = image_at(1 - z, x, parity), right
        elif number == 2:
            image, device = image_at(1 - z, x, parity), left
        else:
            image, device = image_at(z, x + 2, parity), across
        slot = (number - 1) * 2 + parity
        return remote(
            buf.at[image],
            buf.at[image],
            ag_send.at[which, slot],
            ag_recv.at[which, slot],
            device,
        )

    def gather_first(buf, which):
        for number, parity in ((6, 0), (7, 1), (4, 0), (6, 1), (7, 0), (4, 1)):
            gather_copy(buf, which, number, parity).start()

    def gather_second(buf, which):
        for parity, source in ((0, 6), (1, 7)):
            gather_copy(buf, which, source, parity).wait_recv()
            gather_copy(buf, which, 5, parity).start()
        gather_copy(buf, which, 4, 0).wait_recv()
        gather_copy(buf, which, 1, 0).start()
        gather_copy(buf, which, 2, 0).start()

    def gather_third(buf, which):
        gather_copy(buf, which, 4, 1).wait_recv()
        gather_copy(buf, which, 1, 1).start()
        gather_copy(buf, which, 2, 1).start()

    def gather_fourth(buf, which):
        for parity in (0, 1):
            gather_copy(buf, which, 5, parity).wait_recv()
            gather_copy(buf, which, 3, parity).start()

    def gather_last(buf, which):
        for number, parity in (
            (6, 1), (7, 0), (1, 0), (2, 0), (1, 1), (2, 1), (3, 0), (3, 1),
        ):
            gather_copy(buf, which, number, parity).wait_recv()
        for number in range(1, 8):
            for parity in (0, 1):
                gather_copy(buf, which, number, parity).wait_send()

    mine[0].wait()
    swaps[0].wait_recv()
    key_gain = gains_ref[1:2, :]

    def norm_keys(step, carry):
        parity = lax.div(step, subs)
        rows = columns(lax.rem(step, subs), TILE_TOK)
        entries = kraw[parity, rows, :].astype(F32)
        inverse = lax.rsqrt(jnp.mean(entries * entries, axis=-1, keepdims=True) + EPSILON)
        kbuf[chip + parity, rows, :] = (entries * inverse * key_gain).astype(BF16)
        return carry

    lax.fori_loop(0, 2 * subs, norm_keys, 0)
    gather_first(kbuf, 0)

    gcol[...] = jnp.transpose(jnp.broadcast_to(gains_ref[0:1, :], (HEAD_DIM, HEAD_DIM)))
    qgain[...] = jnp.zeros_like(qgain)
    for i in (2, 3):
        mine[i].wait()
        swaps[i].wait_recv()

    def prepare(t, carry):
        rows = columns(t, TEXT_TILE)
        gain_column = gcol[...]
        for h in range(group):
            cols = slice(h * HEAD_DIM, (h + 1) * HEAD_DIM)
            turned = jnp.transpose(q4[rows, cols].astype(F32))
            inverse = lax.rsqrt(jnp.mean(turned * turned, axis=0, keepdims=True) + EPSILON)
            unit = turned * inverse
            normed = unit * gain_column
            ut[t, :, cols] = unit
            rinv[t, :, cols] = inverse
            qnt[t, :, cols] = normed.astype(BF16)
            qn[t, cols, :] = jnp.transpose(normed).astype(BF16)
            cotangent = do4[rows, cols]
            don[t, cols, :] = cotangent
            dot_t[t, :, cols] = jnp.transpose(cotangent.astype(F32)).astype(BF16)

        @pl.when(t == 0)
        def _():
            gather_second(kbuf, 0)

        @pl.when(t == 1)
        def _():
            gather_third(kbuf, 0)

        @pl.when(t == 3)
        def _():
            gather_fourth(kbuf, 0)

        return carry

    lax.fori_loop(0, tile_total, prepare, 0)

    mine[1].wait()
    swaps[1].wait_recv()
    gather_first(vbuf, 1)
    gather_last(kbuf, 0)

    def forward(t, carry):
        slots = reads(t)
        keys = [kbuf[image] for image, _ in slots]
        for pair in range(pairs):
            cols = slice(pair * pair_width, (pair + 1) * pair_width)
            turned = qnt[t, :, cols]
            scratch = sbuf.at[pair % 2]
            peak = jnp.full((1, pair_width), -1e30, F32)
            for r, (_, length) in enumerate(slots):
                scores = dot(keys[r], turned)
                scratch[r * max_tokens : (r + 1) * max_tokens, :] = scores
                for s in range(subs):
                    top = jnp.max(scores[s * TILE_TOK : (s + 1) * TILE_TOK], axis=0, keepdims=True)
                    peak = jnp.maximum(peak, jnp.where(s * TILE_TOK < length, top, -1e30))
            total = jnp.zeros((1, pair_width), F32)
            for r, (_, length) in enumerate(slots):
                for s in range(subs):
                    begin = r * max_tokens + s * TILE_TOK
                    shift = jnp.where(s * TILE_TOK < length, peak, 1e30)
                    powers = jnp.exp2(
                        (scratch[begin : begin + TILE_TOK, :] - shift) * (scale * LOG2E)
                    )
                    scratch[begin : begin + TILE_TOK, :] = powers
                    total = total + jnp.sum(powers, axis=0, keepdims=True)
            inverse = 1.0 / total
            for r in range(READ_MOST * subs):
                begin = r * TILE_TOK
                wbuf[t, begin : begin + TILE_TOK, cols] = (
                    scratch[begin : begin + TILE_TOK, :] * inverse
                ).astype(BF16)
        cotangents = don[t]
        for r in range(READ_MOST):
            rows = slice(r * max_tokens, (r + 1) * max_tokens)
            vslot[t, r] = dot(wbuf[t, rows, :], cotangents)

        @pl.when(t == 1)
        def _():
            gather_second(vbuf, 1)

        @pl.when(t == 2)
        def _():
            gather_third(vbuf, 1)

        @pl.when(t == 3)
        def _():
            gather_fourth(vbuf, 1)

        return carry

    lax.fori_loop(0, tile_total, forward, 0)

    def sum_route(number, parity):
        if number == 1:
            return image_at(1 - z, x - 1, parity), left
        if number == 2:
            return image_at(1 - z, x + 1, parity), right
        if number == 3:
            return image_at(1 - z, x + 2, parity), across
        if number == 4:
            return image_at(1 - z, x, parity), across
        if number == 5:
            return image_at(z, x + 2, parity), (left, right)[parity]
        if number == 6:
            return image_at(z, x - 1, parity), left
        return image_at(z, x + 1, parity), right

    def sum_copy(send, land, which, number, parity):
        image, device = sum_route(number, parity)
        slot = (number - 1) * 2 + parity
        return remote(
            send.at[image], land.at[slot], rs_send.at[which, slot], rs_recv.at[which, slot], device
        )

    def share(slot_ref, image, s):
        rows = slice(s * TILE_TOK, (s + 1) * TILE_TOK)
        value = None
        for t in range(tile_total):
            place = image - first[t]
            weight = jnp.where((place >= 0) & (place < count[t]), 1.0, 0.0).astype(F32)
            part = slot_ref[t, jnp.clip(place, 0, READ_MOST - 1), rows, :] * weight
            value = part if value is None else value + part
        return value

    def summed(slot_ref, land, image, sources, s):
        value = share(slot_ref, image, s)
        for number, parity in sources:
            slot = (number - 1) * 2 + parity
            value = value + land[slot, s * TILE_TOK : (s + 1) * TILE_TOK, :].astype(F32)
        return value

    def send_sum(slot_ref, send, land, which, number, parity, sources):
        for source_number, source_parity in sources:
            sum_copy(send, land, which, source_number, source_parity).wait_recv()
        image, _ = sum_route(number, parity)
        for s in range(subs):
            rows = slice(s * TILE_TOK, (s + 1) * TILE_TOK)
            send[image, rows, :] = summed(slot_ref, land, image, sources, s).astype(BF16)
        sum_copy(send, land, which, number, parity).start()

    def sum_first(*refs):
        for parity in (0, 1):
            for number in (3, 1, 2):
                send_sum(*refs, number, parity, ())
        send_sum(*refs, 6, 1, ())
        send_sum(*refs, 7, 0, ())

    def sum_second(*refs):
        for parity in (0, 1):
            send_sum(*refs, 5, parity, ((3, parity),))
        for parity in (0, 1):
            send_sum(*refs, 4, parity, ((1, parity), (2, parity)))

    def sum_third(*refs):
        send_sum(*refs, 6, 0, ((5, 0),))
        send_sum(*refs, 7, 1, ((5, 1),))

    root_sources = (4, 6, 7)

    def sum_last(send, land, which):
        for number in root_sources:
            for parity in (0, 1):
                sum_copy(send, land, which, number, parity).wait_recv()
        for number in range(1, 8):
            for parity in (0, 1):
                sum_copy(send, land, which, number, parity).wait_send()

    value_refs = (vslot, vsend, vland, 0)
    key_refs = (kslot, ksend, kland, 1)
    sum_first(*value_refs)
    gather_last(vbuf, 1)

    def backward(t, carry):
        slots = reads(t)
        gain_column = gcol[...]
        gain_pair = jnp.concatenate([gain_column, gain_column], axis=1)
        values = [vbuf[image] for image, _ in slots]
        values_turned = [jnp.transpose(value) for value in values]
        keys_turned = [jnp.transpose(kbuf[image]) for image, _ in slots]
        rows_out = columns(t, TEXT_TILE)
        for pair in range(pairs):
            cols = slice(pair * pair_width, (pair + 1) * pair_width)
            cotangent = dot_t[t, :, cols]
            attended = None
            for r in range(READ_MOST):
                part = dot(
                    values_turned[r], wbuf[t, r * max_tokens : (r + 1) * max_tokens, cols]
                )
                attended = part if attended is None else attended + part
            row_dot = jnp.sum(attended * cotangent.astype(F32), axis=0, keepdims=True)
            grads = None
            for r in range(READ_MOST):
                rows = slice(r * max_tokens, (r + 1) * max_tokens)
                value_scores = dot(values[r], cotangent)
                score_grads = (
                    wbuf[t, rows, cols].astype(F32) * (value_scores - row_dot)
                ).astype(BF16)
                wbuf[t, rows, cols] = score_grads
                part = dot(keys_turned[r], score_grads)
                grads = part if grads is None else grads + part
            grads = grads * scale
            unit = ut[t, :, cols]
            scaled = grads * gain_pair
            mean = jnp.mean(scaled * unit, axis=0, keepdims=True)
            grad_query = rinv[t, :, cols] * (scaled - unit * mean)
            qgain[...] += grads * unit
            for h in range(2):
                head = slice(h * HEAD_DIM, (h + 1) * HEAD_DIM)
                out_cols = slice((2 * pair + h) * HEAD_DIM, (2 * pair + h + 1) * HEAD_DIM)
                obuf[rows_out, out_cols] = jnp.transpose(attended[:, head]).astype(BF16)
                dqbuf[rows_out, out_cols] = jnp.transpose(grad_query[:, head]).astype(BF16)
        normed = qn[t]
        for r in range(READ_MOST):
            rows = slice(r * max_tokens, (r + 1) * max_tokens)
            kslot[t, r] = dot(wbuf[t, rows, :], normed)

        @pl.when(t == 1)
        def _():
            sum_second(*value_refs)

        @pl.when(t == 2)
        def _():
            sum_third(*value_refs)

        return carry

    lax.fori_loop(0, tile_total, backward, 0)
    sum_first(*key_refs)

    out_cols = columns(core, half)
    head_cols = columns(core, HEAD_DIM)
    results = [
        (obuf.at[own_rows], obuf.at[other_rows], o_out, out_cols),
        (dqbuf.at[own_rows], dqbuf.at[other_rows], dq_out, out_cols),
        (gvbuf.at[core], gvbuf.at[other], dv_out, head_cols),
        (gkbuf.at[core], gkbuf.at[other], dk_out, head_cols),
    ]
    locals_out = [
        pltpu.make_async_copy(own, out.at[:, cols], out_local.at[i])
        for i, (own, _, out, cols) in enumerate(results)
    ]
    remotes_out = [
        remote(theirs, out.at[:, cols], out_send.at[i], out_recv.at[i], peer)
        for i, (_, theirs, out, cols) in enumerate(results)
    ]

    def put_out(i):
        locals_out[i].start()
        remotes_out[i].start()

    put_out(0)
    put_out(1)

    sum_last(vsend, vland, 0)
    for parity in (0, 1):
        sources = [(number, parity) for number in root_sources]
        for s in range(subs):
            rows = slice(s * TILE_TOK, (s + 1) * TILE_TOK)
            gvbuf[parity, rows, :] = summed(vslot, vland, chip + parity, sources, s).astype(BF16)
    put_out(2)

    sum_second(*key_refs)
    sum_third(*key_refs)
    sum_last(ksend, kland, 1)
    key_total = jnp.zeros((1, HEAD_DIM), F32)
    for parity in (0, 1):
        sources = [(number, parity) for number in root_sources]
        for s in range(subs):
            rows = slice(s * TILE_TOK, (s + 1) * TILE_TOK)
            grads = summed(kslot, kland, chip + parity, sources, s) * scale
            entries = kraw[parity, rows, :].astype(F32)
            inverse = lax.rsqrt(jnp.mean(entries * entries, axis=-1, keepdims=True) + EPSILON)
            unit = entries * inverse
            scaled = grads * key_gain
            mean = jnp.mean(scaled * unit, axis=-1, keepdims=True)
            gkbuf[parity, rows, :] = (inverse * (scaled - unit * mean)).astype(BF16)
            key_total = key_total + jnp.sum(grads * unit, axis=0, keepdims=True)
    put_out(3)
    query_total = jnp.sum(
        jnp.transpose(qgain[:, :HEAD_DIM] + qgain[:, HEAD_DIM:]), axis=0, keepdims=True
    )
    gain_out[...] = jnp.concatenate([query_total, key_total], axis=0)

    for copy in swaps:
        copy.wait_send()
    for i in range(len(results)):
        locals_out[i].wait()
        remotes_out[i].wait_send()
        remotes_out[i].wait_recv()


def on_device(queries, image_keys, image_values, norm_gains, image_tiles, read_mask, grad_attended):
    tokens, width = queries.shape[1:]
    max_tokens, kv_width = image_keys.shape[2:]
    group = width // kv_width
    images = read_mask.shape[2]
    half = group * HEAD_DIM
    tile_total = 2 * tokens // TEXT_TILE
    slot_width = READ_MOST * max_tokens
    hbm = pl.BlockSpec(memory_space=pl.ANY)
    vmem = pl.BlockSpec(memory_space=pltpu.VMEM)
    smem = pl.BlockSpec(memory_space=pltpu.SMEM)
    dma = pltpu.SemaphoreType.DMA
    block = (images, max_tokens, HEAD_DIM)
    slots = (tile_total, READ_MOST, max_tokens, HEAD_DIM)
    turned = (tile_total, HEAD_DIM, half)
    plain = (tile_total, half, HEAD_DIM)
    scratch = [
        pltpu.VMEM((2 * tokens, half), BF16),
        pltpu.VMEM((2 * tokens, half), BF16),
        pltpu.VMEM((2, max_tokens, HEAD_DIM), BF16),
        pltpu.VMEM(block, BF16),
        pltpu.VMEM(block, BF16),
        pltpu.VMEM(plain, BF16),
        pltpu.VMEM(turned, BF16),
        pltpu.VMEM(turned, BF16),
        pltpu.VMEM(plain, BF16),
        pltpu.VMEM(turned, F32),
        pltpu.VMEM((tile_total, 1, half), F32),
        pltpu.VMEM((tile_total, slot_width, half), BF16),
        pltpu.VMEM((2, slot_width, 2 * HEAD_DIM), F32),
        pltpu.VMEM(slots, F32),
        pltpu.VMEM(slots, F32),
        pltpu.VMEM(block, BF16),
        pltpu.VMEM(block, BF16),
        pltpu.VMEM((14, max_tokens, HEAD_DIM), BF16),
        pltpu.VMEM((14, max_tokens, HEAD_DIM), BF16),
        pltpu.VMEM((2 * tokens, half), BF16),
        pltpu.VMEM((2 * tokens, half), BF16),
        pltpu.VMEM((2, max_tokens, HEAD_DIM), BF16),
        pltpu.VMEM((2, max_tokens, HEAD_DIM), BF16),
        pltpu.VMEM((HEAD_DIM, 2 * HEAD_DIM), F32),
        pltpu.VMEM((HEAD_DIM, HEAD_DIM), F32),
        dma((4,)),
        dma((4,)),
        dma((4,)),
        dma((2, 14)),
        dma((2, 14)),
        dma((2, 14)),
        dma((2, 14)),
        dma((4,)),
        dma((4,)),
        dma((4,)),
    ]
    attended, grad_queries, grad_keys, grad_values, gain_parts = pl.pallas_call(
        functools.partial(kernel, images, group),
        out_shape=[
            jax.ShapeDtypeStruct((tokens, width), BF16),
            jax.ShapeDtypeStruct((tokens, width), BF16),
            jax.ShapeDtypeStruct((max_tokens, kv_width), BF16),
            jax.ShapeDtypeStruct((max_tokens, kv_width), BF16),
            jax.ShapeDtypeStruct((2, HEAD_DIM), F32),
        ],
        in_specs=[hbm, hbm, hbm, hbm, vmem, smem, smem],
        out_specs=[hbm, hbm, hbm, hbm, vmem],
        scratch_shapes=scratch,
        compiler_params=pltpu.CompilerParams(
            collective_id=0, has_side_effects=True, vmem_limit_bytes=60 * 1024 * 1024
        ),
    )(
        queries[0],
        grad_attended[0],
        image_keys[0, 0],
        image_values[0, 0],
        norm_gains,
        image_tiles[0],
        read_mask[0],
    )
    grad_gains = lax.psum(gain_parts, ("dp", "seq", "mp"))
    return (
        attended[None],
        grad_queries[None],
        grad_keys[None, None],
        grad_values[None, None],
        grad_gains,
    )


def solution(mesh):
    in_specs = (
        P("dp", "seq", "mp"),
        P("dp", "seq", None, "mp"),
        P("dp", "seq", None, "mp"),
        P(),
        P("dp", None),
        P("dp", None, None),
        P("dp", "seq", "mp"),
    )
    out_specs = (
        P("dp", "seq", "mp"),
        P("dp", "seq", "mp"),
        P("dp", "seq", None, "mp"),
        P("dp", "seq", None, "mp"),
        P(),
    )
    return jax.shard_map(
        on_device, mesh=mesh, in_specs=in_specs, out_specs=out_specs, check_vma=False
    )
```

time: 446 us -> 173 us (0.39); the launches traced: 439 us -> 172 us
  local copies, waits for them, and re-layouts: 150 us -> 7.27 us
  matrix products: 95.5 us -> 0 us
  Pallas kernels: 0 us -> 86.2 us
  other arithmetic: 60.6 us -> 0 us
  waiting for transfers between devices: 34.9 us -> 0 us
  between operations: 14.4 us -> 0.66 us
    dot_general x18 -> x0, matrix products: 95.5 us -> none  [the longest x2 17.2 us: backward_block(): jnp.einsum('tqegd,tked->tegqk', cotangent_block, value_rows, preferred_el...]
    pallas_call x0 -> x1, Pallas kernels: none -> 86.2 us  [on_device(): pl.pallas_call(functools.partial(kernel, images, group), out_shape=[jax.S...]
    while x43 -> x0, local copies, waits for them, and re-layouts: 51 us -> none
    gather x8 -> x0, local copies, waits for them, and re-layouts: 37 us -> none  [slot_rows(): source[chosen_block].reshape(block_tiles, slot_width, kv_local, HEAD_DIM)]
    all_gather x2 -> x0, waiting for transfers between devices: 33.5 us -> none  [the longest x1 32.4 us: on_device(): lax.all_gather(image_keys[0], 'seq', axis=0, tiled=True)]
    reduce_sum x10 -> x0, other arithmetic: 33.3 us -> none  [the longest x4 15.3 us: block_weights(): jnp.sum(exponent, axis=4, keepdims=True)]
    convert_element_type x6 -> x0, other arithmetic: 19.5 us -> none  [the longest x1 13.1 us: on_device(): key_normed = (key_unit_here * norm_gains[1]).astype(jnp.bfloat16)]
    mul x11 -> x0, local copies, waits for them, and re-layouts: 12.9 us -> none  [the longest x2 4.89 us: backward_block(): jnp.einsum('tegqk,tqegd->tked', score_grads, query_block, preferred_eleme...]
  transfers between devices with their start and end apart: 4 -> 0, of which waited for: 2 -> 0; matrix products, arithmetic and copies ran while one was open for 32% -> 0% of each run, Pallas kernels for 0% -> 0%
where the time goes in v1:
time: 173 us; the launch traced here: 172 us
  Pallas kernels  86.2 us (50%)
  blocking collectives  77.9 us (45%)
  local copies, waits for them, and re-layouts  7.27 us (4%)
    pallas_call x1, Pallas kernels, on_device(): pl.pallas_call(functools.partial(kernel, images, group), out_shape=[jax.S...  86.2 us
    psum x1, blocking collectives, on_device(): grad_gains = lax.psum(gain_parts, ('dp', 'seq', 'mp'))  77.9 us
    unnamed x15, local copies, waits for them, and re-layouts  7.27 us

profile of v1, /device:TPU:1, one launch (start us, length us, event | category | flops | bytes accessed | tf_op | source)
XLA Modules:
  0.0 172.1 jit_solution(9393934466285257159)
XLA Ops:
  0.6 0.0 copy-start.3
  0.6 0.7 copy-done.3
  1.3 0.7 copy.12
  2.0 86.2 %shard_map.110 = (bf16[256,2048]{1,0:T(8,128)(2,1)}, bf16[256,2048]{1,0:T(8,128)(2,1)}, bf16[512,256]{1,0:T(8,128)(2,1)}, bf16[512,256]{1,0:T(8,128)(2,1)}, f32[2,128]{1,0:T(2,128)}) custom-call(bf16[256,2048]{1,0:T(8,128)(2,1)} %bitcast.10, bf16[256,2048]{1,0:T(8,128)(2,1)} %bitcast.11, bf16[512,256]{1,0:T(8,128)(2,1)} %bitcast.16, ...), custom_call_target="tpu_custom_call" | custom-call | tf_op jit(solution)/shard_map/pallas_call | solution.py:594
  88.3 0.0 copy-start.4
  88.3 0.7 copy-done.4
  88.9 77.9 %psum.7 = f32[2,128]{1,0:T(2,128)} all-reduce(f32[2,128]{1,0:T(2,128)S(1)} %copy-done.4), channel_id=1, replica_groups=mesh['dp'=4,'seq'=16,'mp'=4] {'dp','seq','mp'}, use_global_device_ids=true, to_apply=%region_0.0 | all-reduce | flops 256 | bytes 2048 | tf_op jit(solution)/shard_map/psum | solution.py:618
  166.9 0.0 copy-start
  166.9 2.4 %copy.17 = bf16[1,256,2048]{2,1,0:T(8,128)(2,1)} copy(bf16[1,256,2048]{2,1,0:T(8,128)(2,1)} %bitcast.13) | data formatting | bytes 2097152
  169.3 0.0 copy-done
  169.3 0.0 copy-start.2
  169.3 1.0 copy.18
  170.2 0.1 copy-done.2
  170.4 0.0 copy-start.1
  170.4 0.7 copy.19
  171.1 0.3 copy-done.1
  171.4 0.7 copy.20
Async XLA Ops:
  0.6 0.7 copy-start.3
  88.3 0.7 copy-start.4
  166.9 2.4 %copy-start = (bf16[256,2048]{1,0:T(8,128)(2,1)S(1)}, bf16[256,2048]{1,0:T(8,128)(2,1)}, u32[]{:S(2)}) copy-start(bf16[256,2048]{1,0:T(8,128)(2,1)} %get-tuple-element.11) | copy-start | bytes 3145732
  169.3 1.1 copy-start.2
  170.4 1.0 copy-start.1

commit v2 on v1

--- a/solution.py
+++ b/solution.py
@@ -27,6 +27,8 @@
 def kernel(
     images,
     group,
+    dp_total,
+    mp_total,
     q_ref,
     do_ref,
     k_ref,
@@ -62,8 +64,13 @@
     dqbuf,
     gkbuf,
     gvbuf,
-    qgain,
+    oturn,
+    overlap,
     gcol,
+    zgain,
+    ygain,
+    cgain,
+    xgain,
     local_sem,
     swap_send,
     swap_recv,
@@ -74,6 +81,14 @@
     out_local,
     out_send,
     out_recv,
+    zsend,
+    zrecv,
+    ysend,
+    yrecv,
+    csend,
+    crecv,
+    xsend,
+    xrecv,
 ):
     max_tokens = k_ref.shape[0]
     tokens = q_ref.shape[0]
@@ -94,6 +109,8 @@
         return zz * (2 * RING) + lax.rem(xx + RING, RING) * 2 + parity
 
     peer = image_at(z, x, other)
+    dp = lax.axis_index("dp")
+    mp = lax.axis_index("mp")
     right = image_at(z, x + 1, core)
     left = image_at(z, x - 1, core)
     across = image_at(1 - z, x, core)
@@ -106,12 +123,13 @@
     other_rows = columns(other, tokens)
 
     def remote(src, dst, send_sem, recv_sem, device):
+        device = device if isinstance(device, dict) else {"seq": device}
         return pltpu.make_async_remote_copy(
             src_ref=src,
             dst_ref=dst,
             send_sem=send_sem,
             recv_sem=recv_sem,
-            device_id={"seq": device},
+            device_id=device,
             device_id_type=MESH,
         )
 
@@ -127,9 +145,25 @@
         copy.start()
 
     barrier = pltpu.get_barrier_semaphore()
-    for device in (peer, right, left, across):
-        pl.semaphore_signal(barrier, inc=1, device_id={"seq": device}, device_id_type=MESH)
-    pl.semaphore_wait(barrier, 4)
+    chain = 2 * mp_total
+
+    def z_device(k):
+        place = lax.rem(2 * mp + z + k, chain)
+        return {"seq": image_at(lax.rem(place, 2), x, core), "mp": lax.div(place, 2)}
+
+    def y_device(k):
+        return {"dp": lax.rem(dp + k, dp_total)}
+
+    def x_device(k):
+        return {"seq": image_at(z, x + k, core)}
+
+    greeted = [{"seq": peer}]
+    greeted += [x_device(k) for k in range(1, RING)]
+    greeted += [y_device(k) for k in range(1, dp_total)]
+    greeted += [z_device(k) for k in range(1, chain)]
+    for device in greeted:
+        pl.semaphore_signal(barrier, inc=1, device_id=device, device_id_type=MESH)
+    pl.semaphore_wait(barrier, len(greeted))
 
     swaps = [
         (k_ref.at[:, columns(other, HEAD_DIM)], kraw.at[core]),
@@ -150,7 +184,7 @@
         begin = jnp.int32(images)
         total = jnp.int32(0)
         for i in range(images):
-            flag = mask_ref[tile_base + t, i]
+            flag = mask_ref[i, tile_base + t]
             total = total + flag
             begin = jnp.where((flag == 1) & (begin == images), i, begin)
         first.append(begin)
@@ -245,7 +279,7 @@
     gather_first(kbuf, 0)
 
     gcol[...] = jnp.transpose(jnp.broadcast_to(gains_ref[0:1, :], (HEAD_DIM, HEAD_DIM)))
-    qgain[...] = jnp.zeros_like(qgain)
+    overlap[...] = jnp.zeros_like(overlap)
     for i in (2, 3):
         mine[i].wait()
         swaps[i].wait_recv()
@@ -267,21 +301,12 @@
             don[t, cols, :] = cotangent
             dot_t[t, :, cols] = jnp.transpose(cotangent.astype(F32)).astype(BF16)
 
-        @pl.when(t == 0)
-        def _():
-            gather_second(kbuf, 0)
-
-        @pl.when(t == 1)
-        def _():
-            gather_third(kbuf, 0)
-
-        @pl.when(t == 3)
-        def _():
-            gather_fourth(kbuf, 0)
-
         return carry
 
     lax.fori_loop(0, tile_total, prepare, 0)
+    gather_second(kbuf, 0)
+    gather_third(kbuf, 0)
+    gather_fourth(kbuf, 0)
 
     mine[1].wait()
     swaps[1].wait_recv()
@@ -323,15 +348,15 @@
             rows = slice(r * max_tokens, (r + 1) * max_tokens)
             vslot[t, r] = dot(wbuf[t, rows, :], cotangents)
 
+        @pl.when(t == 0)
+        def _():
+            gather_second(vbuf, 1)
+
         @pl.when(t == 1)
         def _():
-            gather_second(vbuf, 1)
+            gather_third(vbuf, 1)
 
         @pl.when(t == 2)
-        def _():
-            gather_third(vbuf, 1)
-
-        @pl.when(t == 3)
         def _():
             gather_fourth(vbuf, 1)
 
@@ -421,12 +446,8 @@
 
     def backward(t, carry):
         slots = reads(t)
-        gain_column = gcol[...]
-        gain_pair = jnp.concatenate([gain_column, gain_column], axis=1)
         values = [vbuf[image] for image, _ in slots]
         values_turned = [jnp.transpose(value) for value in values]
-        keys_turned = [jnp.transpose(kbuf[image]) for image, _ in slots]
-        rows_out = columns(t, TEXT_TILE)
         for pair in range(pairs):
             cols = slice(pair * pair_width, (pair + 1) * pair_width)
             cotangent = dot_t[t, :, cols]
@@ -436,45 +457,97 @@
                     values_turned[r], wbuf[t, r * max_tokens : (r + 1) * max_tokens, cols]
                 )
                 attended = part if attended is None else attended + part
+            oturn[t, :, cols] = attended.astype(BF16)
             row_dot = jnp.sum(attended * cotangent.astype(F32), axis=0, keepdims=True)
-            grads = None
             for r in range(READ_MOST):
                 rows = slice(r * max_tokens, (r + 1) * max_tokens)
                 value_scores = dot(values[r], cotangent)
-                score_grads = (
+                wbuf[t, rows, cols] = (
                     wbuf[t, rows, cols].astype(F32) * (value_scores - row_dot)
                 ).astype(BF16)
-                wbuf[t, rows, cols] = score_grads
-                part = dot(keys_turned[r], score_grads)
+        normed = qn[t]
+        for r, (image, _) in enumerate(slots):
+            rows = slice(r * max_tokens, (r + 1) * max_tokens)
+            part = dot(wbuf[t, rows, :], normed)
+            kslot[t, r] = part
+            product = part * kbuf[image].astype(F32)
+            overlap[...] += jnp.sum(product.reshape(max_tokens // 8, 8, HEAD_DIM), axis=0)
+
+        @pl.when(t == 2)
+        def _():
+            sum_second(*value_refs)
+
+        return carry
+
+    lax.fori_loop(0, tile_total, backward, 0)
+
+    def gain_copy(buf, send, recv, place, k, device):
+        return remote(buf.at[place], buf.at[place], send.at[k - 1], recv.at[place], device)
+
+    def gain_start(buf, send, recv, place, total, device_of, value):
+        buf[place] = value
+        for k in range(1, total):
+            gain_copy(buf, send, recv, place, k, device_of(k)).start()
+
+    def gain_finish(buf, send, recv, place, total, device_of):
+        for k in range(1, total):
+            source = lax.rem(place + k, total)
+            gain_copy(buf, send, recv, source, k, device_of(k)).wait_recv()
+        for k in range(1, total):
+            gain_copy(buf, send, recv, place, k, device_of(k)).wait_send()
+        value = buf[0]
+        for k in range(1, total):
+            value = value + buf[k]
+        return value
+
+    z_stage = (zgain, zsend, zrecv, 2 * mp + z, chain, z_device)
+    y_stage = (ygain, ysend, yrecv, dp, dp_total, y_device)
+    core_stage = (cgain, csend, crecv, core, 2, lambda k: {"seq": peer})
+    x_stage = (xgain, xsend, xrecv, x, RING, x_device)
+
+    gain_start(*z_stage, overlap[...])
+    sum_first(*key_refs)
+    sum_third(*value_refs)
+
+    def queries_backward(t, carry):
+        slots = reads(t)
+        gain_column = gcol[...]
+        gain_pair = jnp.concatenate([gain_column, gain_column], axis=1)
+        keys_turned = [jnp.transpose(kbuf[image]) for image, _ in slots]
+        rows_out = columns(t, TEXT_TILE)
+        for pair in range(pairs):
+            cols = slice(pair * pair_width, (pair + 1) * pair_width)
+            grads = None
+            for r in range(READ_MOST):
+                part = dot(keys_turned[r], wbuf[t, r * max_tokens : (r + 1) * max_tokens, cols])
                 grads = part if grads is None else grads + part
             grads = grads * scale
             unit = ut[t, :, cols]
             scaled = grads * gain_pair
             mean = jnp.mean(scaled * unit, axis=0, keepdims=True)
             grad_query = rinv[t, :, cols] * (scaled - unit * mean)
-            qgain[...] += grads * unit
             for h in range(2):
                 head = slice(h * HEAD_DIM, (h + 1) * HEAD_DIM)
                 out_cols = slice((2 * pair + h) * HEAD_DIM, (2 * pair + h + 1) * HEAD_DIM)
-                obuf[rows_out, out_cols] = jnp.transpose(attended[:, head]).astype(BF16)
+                obuf[rows_out, out_cols] = jnp.transpose(oturn[t, :, out_cols])
                 dqbuf[rows_out, out_cols] = jnp.transpose(grad_query[:, head]).astype(BF16)
-        normed = qn[t]
-        for r in range(READ_MOST):
-            rows = slice(r * max_tokens, (r + 1) * max_tokens)
-            kslot[t, r] = dot(wbuf[t, rows, :], normed)
+
+        @pl.when(t == 0)
+        def _():
+            gain_start(*y_stage, gain_finish(*z_stage))
 
         @pl.when(t == 1)
         def _():
-            sum_second(*value_refs)
+            gain_start(*core_stage, gain_finish(*y_stage))
 
         @pl.when(t == 2)
         def _():
-            sum_third(*value_refs)
+            gain_start(*x_stage, gain_finish(*core_stage))
+            sum_second(*key_refs)
 
         return carry
 
-    lax.fori_loop(0, tile_total, backward, 0)
-    sum_first(*key_refs)
+    lax.fori_loop(0, tile_total, queries_backward, 0)
 
     out_cols = columns(core, half)
     head_cols = columns(core, HEAD_DIM)
@@ -508,10 +581,8 @@
             gvbuf[parity, rows, :] = summed(vslot, vland, chip + parity, sources, s).astype(BF16)
     put_out(2)
 
-    sum_second(*key_refs)
     sum_third(*key_refs)
     sum_last(ksend, kland, 1)
-    key_total = jnp.zeros((1, HEAD_DIM), F32)
     for parity in (0, 1):
         sources = [(number, parity) for number in root_sources]
         for s in range(subs):
@@ -523,12 +594,9 @@
             scaled = grads * key_gain
             mean = jnp.mean(scaled * unit, axis=-1, keepdims=True)
             gkbuf[parity, rows, :] = (inverse * (scaled - unit * mean)).astype(BF16)
-            key_total = key_total + jnp.sum(grads * unit, axis=0, keepdims=True)
     put_out(3)
-    query_total = jnp.sum(
-        jnp.transpose(qgain[:, :HEAD_DIM] + qgain[:, HEAD_DIM:]), axis=0, keepdims=True
-    )
-    gain_out[...] = jnp.concatenate([query_total, key_total], axis=0)
+    products = jnp.sum(gain_finish(*x_stage), axis=0, keepdims=True) * scale
+    gain_out[...] = products / gains_ref[...]
 
     for copy in swaps:
         copy.wait_send()
@@ -538,7 +606,17 @@
         remotes_out[i].wait_recv()
 
 
-def on_device(queries, image_keys, image_values, norm_gains, image_tiles, read_mask, grad_attended):
+def on_device(
+    dp_total,
+    mp_total,
+    queries,
+    image_keys,
+    image_values,
+    norm_gains,
+    image_tiles,
+    read_mask,
+    grad_attended,
+):
     tokens, width = queries.shape[1:]
     max_tokens, kv_width = image_keys.shape[2:]
     group = width // kv_width
@@ -578,8 +656,13 @@
         pltpu.VMEM((2 * tokens, half), BF16),
         pltpu.VMEM((2, max_tokens, HEAD_DIM), BF16),
         pltpu.VMEM((2, max_tokens, HEAD_DIM), BF16),
-        pltpu.VMEM((HEAD_DIM, 2 * HEAD_DIM), F32),
+        pltpu.VMEM(turned, BF16),
+        pltpu.VMEM((8, HEAD_DIM), F32),
         pltpu.VMEM((HEAD_DIM, HEAD_DIM), F32),
+        pltpu.VMEM((2 * mp_total, 8, HEAD_DIM), F32),
+        pltpu.VMEM((dp_total, 8, HEAD_DIM), F32),
+        pltpu.VMEM((2, 8, HEAD_DIM), F32),
+        pltpu.VMEM((RING, 8, HEAD_DIM), F32),
         dma((4,)),
         dma((4,)),
         dma((4,)),
@@ -590,9 +673,17 @@
         dma((4,)),
         dma((4,)),
         dma((4,)),
+        dma((2 * mp_total,)),
+        dma((2 * mp_total,)),
+        dma((dp_total,)),
+        dma((dp_total,)),
+        dma((2,)),
+        dma((2,)),
+        dma((RING,)),
+        dma((RING,)),
     ]
-    attended, grad_queries, grad_keys, grad_values, gain_parts = pl.pallas_call(
-        functools.partial(kernel, images, group),
+    attended, grad_queries, grad_keys, grad_values, grad_gains = pl.pallas_call(
+        functools.partial(kernel, images, group, dp_total, mp_total),
         out_shape=[
             jax.ShapeDtypeStruct((tokens, width), BF16),
             jax.ShapeDtypeStruct((tokens, width), BF16),
@@ -613,9 +704,8 @@
         image_values[0, 0],
         norm_gains,
         image_tiles[0],
-        read_mask[0],
+        jnp.transpose(read_mask[0]),
     )
-    grad_gains = lax.psum(gain_parts, ("dp", "seq", "mp"))
     return (
         attended[None],
         grad_queries[None],
@@ -642,6 +732,7 @@
         P("dp", "seq", None, "mp"),
         P(),
     )
+    per_device = functools.partial(on_device, mesh.shape["dp"], mesh.shape["mp"])
     return jax.shard_map(
-        on_device, mesh=mesh, in_specs=in_specs, out_specs=out_specs, check_vma=False
+        per_device, mesh=mesh, in_specs=in_specs, out_specs=out_specs, check_vma=False
     )

time: 173 us -> 94.1 us (0.54)
  blocking collectives: 77.9 us -> 0 us
    psum x1 -> x0, blocking collectives: 77.9 us -> none  [on_device(): grad_gains = lax.psum(gain_parts, ('dp', 'seq', 'mp'))]
    unnamed x15 -> x13, local copies, waits for them, and re-layouts: 7.27 us -> 5.8 us
where the time goes in v2:
time: 94.1 us; the launch traced here: 93.9 us
  Pallas kernels  87.4 us (93%)
  local copies, waits for them, and re-layouts  5.8 us (6%)
    pallas_call x1, Pallas kernels, on_device(): pl.pallas_call(functools.partial(kernel, images, group, dp_total, mp_tota...  87.4 us
    unnamed x13, local copies, waits for them, and re-layouts  5.8 us

profile of v2, /device:TPU:1, one launch (start us, length us, event | category | flops | bytes accessed | tf_op | source)
XLA Modules:
  0.0 93.9 jit_solution(12200217997765763315)
XLA Ops:
  0.6 87.4 %shard_map.110 = (bf16[256,2048]{1,0:T(8,128)(2,1)}, bf16[256,2048]{1,0:T(8,128)(2,1)}, bf16[512,256]{1,0:T(8,128)(2,1)}, bf16[512,256]{1,0:T(8,128)(2,1)}, f32[2,128]{1,0:T(2,128)}) custom-call(bf16[256,2048]{1,0:T(8,128)(2,1)} %bitcast.12, bf16[256,2048]{1,0:T(8,128)(2,1)} %bitcast.13, bf16[512,256]{1,0:T(8,128)(2,1)} %bitcast.18, ...), custom_call_target="tpu_custom_call" | custom-call | tf_op jit(solution)/shard_map/pallas_call | solution.py:685
  88.1 0.0 copy-start
  88.1 2.4 %copy.17 = bf16[1,256,2048]{2,1,0:T(8,128)(2,1)} copy(bf16[1,256,2048]{2,1,0:T(8,128)(2,1)} %bitcast.15) | data formatting | bytes 2097152
  90.5 0.0 copy-done
  90.5 0.0 copy-start.2
  90.5 1.0 %copy.18 = bf16[1,256,2048]{2,1,0:T(8,128)(2,1)} copy(bf16[1,256,2048]{2,1,0:T(8,128)(2,1)S(1)} %bitcast.14) | data formatting | bytes 2097152
  91.4 0.1 copy-done.2
  91.5 0.0 copy-start.1
  91.6 0.7 copy.19
  92.3 0.3 copy-done.1
  92.6 0.0 copy-start.3
  92.6 0.7 copy.20
  93.3 0.0 copy-done.3
  93.3 0.6 copy.21
Async XLA Ops:
  88.1 2.4 %copy-start = (bf16[256,2048]{1,0:T(8,128)(2,1)S(1)}, bf16[256,2048]{1,0:T(8,128)(2,1)}, u32[]{:S(2)}) copy-start(bf16[256,2048]{1,0:T(8,128)(2,1)} %get-tuple-element.11) | copy-start | bytes 3145732
  90.5 1.1 %copy-start.2 = (bf16[512,256]{1,0:T(8,128)(2,1)S(1)}, bf16[512,256]{1,0:T(8,128)(2,1)}, u32[]{:S(2)}) copy-start(bf16[512,256]{1,0:T(8,128)(2,1)} %get-tuple-element.12) | copy-start | bytes 786436
  91.5 1.0 %copy-start.1 = (bf16[512,256]{1,0:T(8,128)(2,1)S(1)}, bf16[512,256]{1,0:T(8,128)(2,1)}, u32[]{:S(2)}) copy-start(bf16[512,256]{1,0:T(8,128)(2,1)} %get-tuple-element.13) | copy-start | bytes 786436
  92.6 0.7 copy-start.3

commit v3 on v2

--- a/solution.py
+++ b/solution.py
@@ -15,6 +15,7 @@
 LOG2E = 1.4426950408889634
 MESH = pl.DeviceIdType.MESH
 BF16 = jnp.bfloat16
+MOVE_CUTS = 4
 F32 = jnp.float32
 
 RING = 4
@@ -64,6 +65,9 @@
     dqbuf,
     gkbuf,
     gvbuf,
+    early,
+    unit_keys,
+    inverse_keys,
     oturn,
     overlap,
     gcol,
@@ -133,6 +137,26 @@
             device_id_type=MESH,
         )
 
+    barrier = pltpu.get_barrier_semaphore()
+    chain = 2 * mp_total
+
+    def z_device(k):
+        place = lax.rem(2 * mp + z + k, chain)
+        return {"seq": image_at(lax.rem(place, 2), x, core), "mp": lax.div(place, 2)}
+
+    def y_device(k):
+        return {"dp": lax.rem(dp + k, dp_total)}
+
+    def x_device(k):
+        return {"seq": image_at(z, x + k, core)}
+
+    greeted = [{"seq": peer}]
+    greeted += [x_device(k) for k in range(1, RING)]
+    greeted += [y_device(k) for k in range(1, dp_total)]
+    greeted += [z_device(k) for k in range(1, chain)]
+    for device in greeted:
+        pl.semaphore_signal(barrier, inc=1, device_id=device, device_id_type=MESH)
+
     mine = [
         pltpu.make_async_copy(k_ref.at[:, columns(core, HEAD_DIM)], kraw.at[core], local_sem.at[0]),
         pltpu.make_async_copy(
@@ -144,27 +168,6 @@
     for copy in mine:
         copy.start()
 
-    barrier = pltpu.get_barrier_semaphore()
-    chain = 2 * mp_total
-
-    def z_device(k):
-        place = lax.rem(2 * mp + z + k, chain)
-        return {"seq": image_at(lax.rem(place, 2), x, core), "mp": lax.div(place, 2)}
-
-    def y_device(k):
-        return {"dp": lax.rem(dp + k, dp_total)}
-
-    def x_device(k):
-        return {"seq": image_at(z, x + k, core)}
-
-    greeted = [{"seq": peer}]
-    greeted += [x_device(k) for k in range(1, RING)]
-    greeted += [y_device(k) for k in range(1, dp_total)]
-    greeted += [z_device(k) for k in range(1, chain)]
-    for device in greeted:
-        pl.semaphore_signal(barrier, inc=1, device_id=device, device_id_type=MESH)
-    pl.semaphore_wait(barrier, len(greeted))
-
     swaps = [
         (k_ref.at[:, columns(other, HEAD_DIM)], kraw.at[core]),
         (v_ref.at[:, columns(other, HEAD_DIM)], vbuf.at[chip + core]),
@@ -175,8 +178,6 @@
         remote(src, dst, swap_send.at[i], swap_recv.at[i], peer)
         for i, (src, dst) in enumerate(swaps)
     ]
-    for copy in swaps:
-        copy.start()
 
     tile_base = lax.div(seq, 2) * tile_total
     first, count = [], []
@@ -206,23 +207,7 @@
             found.append((image, length))
         return found
 
-    def gather_copy(buf, which, number, parity):
-        if number == 6:
-            image, device = image_at(z, x, parity), right
-        elif number == 7:
-            image, device = image_at(z, x, parity), left
-        elif number == 4:
-            image, device = image_at(z, x, parity), across
-        elif number == 5 and parity == 0:
-            image, device = image_at(z, x - 1, 0), right
-        elif number == 5:
-            image, device = image_at(z, x + 1, 1), left
-        elif number == 1:
-            image, device = image_at(1 - z, x, parity), right
-        elif number == 2:
-            image, device = image_at(1 - z, x, parity), left
-        else:
-            image, device = image_at(z, x + 2, parity), across
+    def gather_message(buf, which, number, parity, image, device):
         slot = (number - 1) * 2 + parity
         return remote(
             buf.at[image],
@@ -232,51 +217,96 @@
             device,
         )
 
-    def gather_first(buf, which):
-        for number, parity in ((6, 0), (7, 1), (4, 0), (6, 1), (7, 0), (4, 1)):
-            gather_copy(buf, which, number, parity).start()
+    ahead = jnp.where(core == 0, right, left)
+    behind = jnp.where(core == 0, left, right)
+
+    def gather_ahead(buf, which, parity):
+        return gather_message(buf, which, 6 + core, parity, chip + parity, ahead)
+
+    def gather_behind(buf, which, parity):
+        return gather_message(buf, which, 7 - core, parity, chip + parity, behind)
+
+    def gather_across(buf, which, parity):
+        return gather_message(buf, which, 4, parity, chip + parity, across)
+
+    def gather_beside(buf, which, parity):
+        device = jnp.where(parity == 0, left, right)
+        return gather_message(buf, which, 1, parity, image_at(1 - z, x, parity), device)
+
+    def gather_copy(buf, which, number, parity):
+        if number == 6:
+            image, device = image_at(z, x, parity), right
+        elif number == 7:
+            image, device = image_at(z, x, parity), left
+        elif number == 4:
+            image, device = image_at(z, x, parity), across
+        elif number == 5:
+            image, device = image_at(z, x - 1 + 2 * parity, parity), (right, left)[parity]
+        elif number == 3:
+            image, device = image_at(z, x - 1 + 2 * parity, parity), across
+        elif number == 1:
+            image, device = image_at(1 - z, x, parity), (left, right)[parity]
+        else:
+            image, device = image_at(1 - z, x + 1 - 2 * parity, parity), (left, right)[parity]
+        return gather_message(buf, which, number, parity, image, device)
+
+    def gather_own(buf, which):
+        gather_ahead(buf, which, core).start()
+        gather_across(buf, which, core).start()
+
+    def gather_swapped(buf, which):
+        gather_behind(buf, which, other).start()
+        gather_across(buf, which, other).start()
+        gather_ahead(buf, which, other).start()
+        gather_behind(buf, which, core).start()
 
     def gather_second(buf, which):
+        for parity in (core, other):
+            gather_across(buf, which, parity).wait_recv()
+            gather_beside(buf, which, parity).start()
+
+    def gather_third(buf, which):
         for parity, source in ((0, 6), (1, 7)):
             gather_copy(buf, which, source, parity).wait_recv()
             gather_copy(buf, which, 5, parity).start()
-        gather_copy(buf, which, 4, 0).wait_recv()
-        gather_copy(buf, which, 1, 0).start()
-        gather_copy(buf, which, 2, 0).start()
-
-    def gather_third(buf, which):
-        gather_copy(buf, which, 4, 1).wait_recv()
-        gather_copy(buf, which, 1, 1).start()
-        gather_copy(buf, which, 2, 1).start()
+            gather_copy(buf, which, 3, parity).start()
 
     def gather_fourth(buf, which):
         for parity in (0, 1):
-            gather_copy(buf, which, 5, parity).wait_recv()
-            gather_copy(buf, which, 3, parity).start()
+            gather_copy(buf, which, 1, parity).wait_recv()
+            gather_copy(buf, which, 2, parity).start()
 
     def gather_last(buf, which):
         for number, parity in (
-            (6, 1), (7, 0), (1, 0), (2, 0), (1, 1), (2, 1), (3, 0), (3, 1),
+            (6, 1), (7, 0), (5, 0), (5, 1), (3, 0), (3, 1), (2, 0), (2, 1),
         ):
             gather_copy(buf, which, number, parity).wait_recv()
         for number in range(1, 8):
             for parity in (0, 1):
                 gather_copy(buf, which, number, parity).wait_send()
 
+    key_gain = gains_ref[1:2, :]
+
+    def norm_keys(parity):
+        for s in range(subs):
+            rows = slice(s * TILE_TOK, (s + 1) * TILE_TOK)
+            entries = kraw[parity, rows, :].astype(F32)
+            inverse = lax.rsqrt(jnp.mean(entries * entries, axis=-1, keepdims=True) + EPSILON)
+            unit = entries * inverse
+            unit_keys[parity, rows, :] = unit
+            inverse_keys[parity, rows, :] = inverse
+            kbuf[chip + parity, rows, :] = (unit * key_gain).astype(BF16)
+
     mine[0].wait()
+    norm_keys(core)
+    pl.semaphore_wait(barrier, len(greeted))
+    swaps[0].start()
+    gather_own(kbuf, 0)
+    for copy in swaps[1:]:
+        copy.start()
     swaps[0].wait_recv()
-    key_gain = gains_ref[1:2, :]
-
-    def norm_keys(step, carry):
-        parity = lax.div(step, subs)
-        rows = columns(lax.rem(step, subs), TILE_TOK)
-        entries = kraw[parity, rows, :].astype(F32)
-        inverse = lax.rsqrt(jnp.mean(entries * entries, axis=-1, keepdims=True) + EPSILON)
-        kbuf[chip + parity, rows, :] = (entries * inverse * key_gain).astype(BF16)
-        return carry
-
-    lax.fori_loop(0, 2 * subs, norm_keys, 0)
-    gather_first(kbuf, 0)
+    norm_keys(other)
+    gather_swapped(kbuf, 0)
 
     gcol[...] = jnp.transpose(jnp.broadcast_to(gains_ref[0:1, :], (HEAD_DIM, HEAD_DIM)))
     overlap[...] = jnp.zeros_like(overlap)
@@ -310,7 +340,8 @@
 
     mine[1].wait()
     swaps[1].wait_recv()
-    gather_first(vbuf, 1)
+    gather_own(vbuf, 1)
+    gather_swapped(vbuf, 1)
     gather_last(kbuf, 0)
 
     def forward(t, carry):
@@ -351,9 +382,6 @@
         @pl.when(t == 0)
         def _():
             gather_second(vbuf, 1)
-
-        @pl.when(t == 1)
-        def _():
             gather_third(vbuf, 1)
 
         @pl.when(t == 2)
@@ -366,11 +394,11 @@
 
     def sum_route(number, parity):
         if number == 1:
-            return image_at(1 - z, x - 1, parity), left
+            return image_at(1 - z, x + 1 - 2 * parity, parity), (right, left)[parity]
         if number == 2:
-            return image_at(1 - z, x + 1, parity), right
+            return image_at(1 - z, x + 2, parity), (right, left)[parity]
         if number == 3:
-            return image_at(1 - z, x + 2, parity), across
+            return image_at(1 - z, x - 1 + 2 * parity, parity), across
         if number == 4:
             return image_at(1 - z, x, parity), across
         if number == 5:
@@ -412,36 +440,50 @@
             send[image, rows, :] = summed(slot_ref, land, image, sources, s).astype(BF16)
         sum_copy(send, land, which, number, parity).start()
 
-    def sum_first(*refs):
-        for parity in (0, 1):
-            for number in (3, 1, 2):
-                send_sum(*refs, number, parity, ())
+    def sum_far(*refs):
+        send_sum(*refs, 2, 0, ())
+        send_sum(*refs, 2, 1, ())
+
+    def sum_level(*refs):
+        send_sum(*refs, 3, 0, ())
+        send_sum(*refs, 3, 1, ())
+
+    def sum_middle(*refs):
+        send_sum(*refs, 5, 0, ())
+        send_sum(*refs, 5, 1, ())
+
+    def sum_beside(*refs):
+        send_sum(*refs, 1, 0, ((2, 0),))
+        send_sum(*refs, 1, 1, ((2, 1),))
+
+    def sum_near(*refs):
+        send_sum(*refs, 7, 0, ())
         send_sum(*refs, 6, 1, ())
-        send_sum(*refs, 7, 0, ())
-
-    def sum_second(*refs):
-        for parity in (0, 1):
-            send_sum(*refs, 5, parity, ((3, parity),))
-        for parity in (0, 1):
-            send_sum(*refs, 4, parity, ((1, parity), (2, parity)))
-
-    def sum_third(*refs):
-        send_sum(*refs, 6, 0, ((5, 0),))
-        send_sum(*refs, 7, 1, ((5, 1),))
+
+    def sum_across(*refs):
+        send_sum(*refs, 4, 0, ((1, 0),))
+        send_sum(*refs, 4, 1, ((1, 1),))
+
+    def sum_end(*refs):
+        send_sum(*refs, 6, 0, ((5, 0), (3, 0)))
+        send_sum(*refs, 7, 1, ((5, 1), (3, 1)))
 
     root_sources = (4, 6, 7)
 
-    def sum_last(send, land, which):
-        for number in root_sources:
-            for parity in (0, 1):
-                sum_copy(send, land, which, number, parity).wait_recv()
+    root_messages = [(number, parity) for number in root_sources for parity in (0, 1)]
+
+    def sum_last(send, land, which, arriving):
+        for number, parity in arriving:
+            sum_copy(send, land, which, number, parity).wait_recv()
         for number in range(1, 8):
             for parity in (0, 1):
                 sum_copy(send, land, which, number, parity).wait_send()
 
     value_refs = (vslot, vsend, vland, 0)
     key_refs = (kslot, ksend, kland, 1)
-    sum_first(*value_refs)
+    sum_far(*value_refs)
+    sum_level(*value_refs)
+    sum_middle(*value_refs)
     gather_last(vbuf, 1)
 
     def backward(t, carry):
@@ -473,9 +515,10 @@
             product = part * kbuf[image].astype(F32)
             overlap[...] += jnp.sum(product.reshape(max_tokens // 8, 8, HEAD_DIM), axis=0)
 
-        @pl.when(t == 2)
+        @pl.when(t == 0)
         def _():
-            sum_second(*value_refs)
+            sum_beside(*value_refs)
+            sum_near(*value_refs)
 
         return carry
 
@@ -506,8 +549,10 @@
     x_stage = (xgain, xsend, xrecv, x, RING, x_device)
 
     gain_start(*z_stage, overlap[...])
-    sum_first(*key_refs)
-    sum_third(*value_refs)
+    sum_far(*key_refs)
+    sum_end(*value_refs)
+    sum_across(*value_refs)
+    sum_level(*key_refs)
 
     def queries_backward(t, carry):
         slots = reads(t)
@@ -532,18 +577,16 @@
                 obuf[rows_out, out_cols] = jnp.transpose(oturn[t, :, out_cols])
                 dqbuf[rows_out, out_cols] = jnp.transpose(grad_query[:, head]).astype(BF16)
 
-        @pl.when(t == 0)
-        def _():
-            gain_start(*y_stage, gain_finish(*z_stage))
-
         @pl.when(t == 1)
         def _():
+            sum_beside(*key_refs)
+            sum_middle(*key_refs)
+            sum_near(*key_refs)
+            gain_start(*y_stage, gain_finish(*z_stage))
+
+        @pl.when(t == 3)
+        def _():
             gain_start(*core_stage, gain_finish(*y_stage))
-
-        @pl.when(t == 2)
-        def _():
-            gain_start(*x_stage, gain_finish(*core_stage))
-            sum_second(*key_refs)
 
         return carry
 
@@ -573,28 +616,42 @@
     put_out(0)
     put_out(1)
 
-    sum_last(vsend, vland, 0)
-    for parity in (0, 1):
+    def root_sum(slot_ref, land, parity, s):
         sources = [(number, parity) for number in root_sources]
+        return summed(slot_ref, land, chip + parity, sources, s)
+
+    sum_last(vsend, vland, 0, root_messages)
+    for parity in (other, core):
         for s in range(subs):
             rows = slice(s * TILE_TOK, (s + 1) * TILE_TOK)
-            gvbuf[parity, rows, :] = summed(vslot, vland, chip + parity, sources, s).astype(BF16)
+            gvbuf[parity, rows, :] = root_sum(vslot, vland, parity, s).astype(BF16)
     put_out(2)
 
-    sum_third(*key_refs)
-    sum_last(ksend, kland, 1)
-    for parity in (0, 1):
-        sources = [(number, parity) for number in root_sources]
+    sum_across(*key_refs)
+    gain_start(*x_stage, gain_finish(*core_stage))
+    sum_end(*key_refs)
+    for number, parity in ((7, 0), (6, 1)):
+        sum_copy(ksend, kland, 1, number, parity).wait_recv()
         for s in range(subs):
             rows = slice(s * TILE_TOK, (s + 1) * TILE_TOK)
-            grads = summed(kslot, kland, chip + parity, sources, s) * scale
-            entries = kraw[parity, rows, :].astype(F32)
-            inverse = lax.rsqrt(jnp.mean(entries * entries, axis=-1, keepdims=True) + EPSILON)
-            unit = entries * inverse
+            early[parity, rows, :] = summed(kslot, kland, chip + parity, [(number, parity)], s)
+    sum_last(ksend, kland, 1, ((4, 0), (4, 1), (6, 0), (7, 1)))
+    for parity in (other, core):
+        for s in range(subs):
+            rows = slice(s * TILE_TOK, (s + 1) * TILE_TOK)
+            grads = early[parity, rows, :]
+            for slot in (6 + parity, 10 + 3 * parity):
+                grads = grads + kland[slot, rows, :].astype(F32)
+            grads = grads * scale
+            unit = unit_keys[parity, rows, :]
             scaled = grads * key_gain
             mean = jnp.mean(scaled * unit, axis=-1, keepdims=True)
-            gkbuf[parity, rows, :] = (inverse * (scaled - unit * mean)).astype(BF16)
-    put_out(3)
+            gkbuf[parity, rows, :] = (
+                inverse_keys[parity, rows, :] * (scaled - unit * mean)
+            ).astype(BF16)
+        if parity is other:
+            remotes_out[3].start()
+    locals_out[3].start()
     products = jnp.sum(gain_finish(*x_stage), axis=0, keepdims=True) * scale
     gain_out[...] = products / gains_ref[...]
 
@@ -604,6 +661,27 @@
         locals_out[i].wait()
         remotes_out[i].wait_send()
         remotes_out[i].wait_recv()
+
+
+def mover(count, *refs):
+    sources, targets = refs[:count], refs[count : 2 * count]
+    stages, load_sem, store_sem = refs[2 * count : 3 * count], refs[-2], refs[-1]
+    loads, stores = [], []
+    for source, stage, target in zip(sources, stages, targets):
+        cuts = MOVE_CUTS if source.shape[0] % (16 * MOVE_CUTS) == 0 else 1
+        rows = source.shape[0] // cuts
+        for k in range(cuts):
+            cut = pl.ds(k * rows, rows)
+            place = len(loads)
+            loads.append(pltpu.make_async_copy(source.at[cut], stage.at[cut], load_sem.at[place]))
+            stores.append(pltpu.make_async_copy(stage.at[cut], target.at[cut], store_sem.at[place]))
+    for load in loads:
+        load.start()
+    for load, store in zip(loads, stores):
+        load.wait()
+        store.start()
+    for store in stores:
+        store.wait()
 
 
 def on_device(
@@ -656,6 +734,9 @@
         pltpu.VMEM((2 * tokens, half), BF16),
         pltpu.VMEM((2, max_tokens, HEAD_DIM), BF16),
         pltpu.VMEM((2, max_tokens, HEAD_DIM), BF16),
+        pltpu.VMEM((2, max_tokens, HEAD_DIM), F32),
+        pltpu.VMEM((2, max_tokens, HEAD_DIM), F32),
+        pltpu.VMEM((2, max_tokens, 1), F32),
         pltpu.VMEM(turned, BF16),
         pltpu.VMEM((8, HEAD_DIM), F32),
         pltpu.VMEM((HEAD_DIM, HEAD_DIM), F32),
@@ -706,6 +787,16 @@
         image_tiles[0],
         jnp.transpose(read_mask[0]),
     )
+    results = (attended, grad_queries, grad_keys, grad_values, grad_gains)
+    attended, grad_queries, grad_keys, grad_values, grad_gains = pl.pallas_call(
+        functools.partial(mover, len(results)),
+        out_shape=[jax.ShapeDtypeStruct(part.shape, part.dtype) for part in results],
+        in_specs=[hbm] * len(results),
+        out_specs=[hbm] * len(results),
+        scratch_shapes=[pltpu.VMEM(part.shape, part.dtype) for part in results]
+        + [dma((MOVE_CUTS * len(results),))] * 2,
+        compiler_params=pltpu.CompilerParams(vmem_limit_bytes=60 * 1024 * 1024),
+    )(*results)
     return (
         attended[None],
         grad_queries[None],

time: 94.1 us -> 81.1 us (0.86)
  Pallas kernels: 87.4 us -> 80.2 us
  local copies, waits for them, and re-layouts: 5.8 us -> 0 us
    pallas_call x1, Pallas kernels: 87.4 us -> 77.5 us  [on_device(): pl.pallas_call(functools.partial(kernel, images, group, dp_total, mp_tota...]
    unnamed x13 -> x0, local copies, waits for them, and re-layouts: 5.8 us -> none
    pallas_call x0 -> x1, Pallas kernels: none -> 2.77 us  [on_device(): pl.pallas_call(functools.partial(mover, len(results)), out_shape=[jax.Sha...]
where the time goes in v3:
time: 81.1 us; the launch traced here: 80.9 us
  Pallas kernels  80.2 us (99%)
    pallas_call x1, Pallas kernels, on_device(): pl.pallas_call(functools.partial(kernel, images, group, dp_total, mp_tota...  77.5 us
    pallas_call x1, Pallas kernels, on_device(): pl.pallas_call(functools.partial(mover, len(results)), out_shape=[jax.Sha...  2.77 us

profile of v3, /device:TPU:1, one launch (start us, length us, event | category | flops | bytes accessed | tf_op | source)
XLA Modules:
  0.0 80.9 jit_solution(5314536020815364287)
XLA Ops:
  0.6 77.5 %shard_map.110 = (bf16[256,2048]{1,0:T(8,128)(2,1)}, bf16[256,2048]{1,0:T(8,128)(2,1)}, bf16[512,256]{1,0:T(8,128)(2,1)}, bf16[512,256]{1,0:T(8,128)(2,1)}, f32[2,128]{1,0:T(2,128)}) custom-call(bf16[256,2048]{1,0:T(8,128)(2,1)} %bitcast.12, bf16[256,2048]{1,0:T(8,128)(2,1)} %bitcast.13, bf16[512,256]{1,0:T(8,128)(2,1)} %bitcast.14, ...), custom_call_target="tpu_custom_call" | custom-call | tf_op jit(solution)/shard_map/pallas_call | solution.py:766
  78.1 2.8 %shard_map.111 = (bf16[256,2048]{1,0:T(8,128)(2,1)}, bf16[256,2048]{1,0:T(8,128)(2,1)}, bf16[512,256]{1,0:T(8,128)(2,1)}, bf16[512,256]{1,0:T(8,128)(2,1)}, f32[2,128]{1,0:T(2,128)}) custom-call(bf16[256,2048]{1,0:T(8,128)(2,1)} %get-tuple-element.15.refs_0_, bf16[256,2048]{1,0:T(8,128)(2,1)} %get-tuple-element.16.refs_1_, ...), custom_call_target="tpu_custom_call" | custom-call | tf_op jit(solution)/shard_map/pallas_call | solution.py:791

commit v4 on v3

--- a/solution.py
+++ b/solution.py
@@ -71,10 +71,9 @@
     oturn,
     overlap,
     gcol,
-    zgain,
-    ygain,
-    cgain,
-    xgain,
+    member_gain,
+    cross_gain,
+    total_gain,
     local_sem,
     swap_send,
     swap_recv,
@@ -85,14 +84,13 @@
     out_local,
     out_send,
     out_recv,
-    zsend,
-    zrecv,
-    ysend,
-    yrecv,
-    csend,
-    crecv,
-    xsend,
-    xrecv,
+    ready_sem,
+    member_send,
+    member_recv,
+    cross_send,
+    cross_recv,
+    total_send,
+    total_recv,
 ):
     max_tokens = k_ref.shape[0]
     tokens = q_ref.shape[0]
@@ -138,24 +136,43 @@
         )
 
     barrier = pltpu.get_barrier_semaphore()
-    chain = 2 * mp_total
-
-    def z_device(k):
-        place = lax.rem(2 * mp + z + k, chain)
-        return {"seq": image_at(lax.rem(place, 2), x, core), "mp": lax.div(place, 2)}
-
-    def y_device(k):
-        return {"dp": lax.rem(dp + k, dp_total)}
-
-    def x_device(k):
-        return {"seq": image_at(z, x + k, core)}
-
-    greeted = [{"seq": peer}]
-    greeted += [x_device(k) for k in range(1, RING)]
-    greeted += [y_device(k) for k in range(1, dp_total)]
-    greeted += [z_device(k) for k in range(1, chain)]
-    for device in greeted:
-        pl.semaphore_signal(barrier, inc=1, device_id=device, device_id_type=MESH)
+    leader = seq == 0
+    members = 2 * 2 * RING
+    group_total = dp_total * mp_total
+    group_place = dp * mp_total + mp
+
+    def cross_device(k):
+        place = lax.rem(group_place + k, group_total)
+        return {"dp": lax.div(place, mp_total), "mp": lax.rem(place, mp_total)}
+
+    neighbours = (peer, right, left, across)
+    for device in neighbours:
+
+        @pl.when(device != 0)
+        def _():
+            pl.semaphore_signal(barrier, inc=1, device_id={"seq": device}, device_id_type=MESH)
+
+    @pl.when(leader)
+    def _():
+        for k in range(1, group_total):
+            pl.semaphore_signal(barrier, inc=1, device_id=cross_device(k), device_id_type=MESH)
+
+    def enter():
+        @pl.when(leader)
+        def _():
+            pl.semaphore_wait(ready_sem, len(neighbours))
+
+        @pl.when(jnp.logical_not(leader))
+        def _():
+            pl.semaphore_wait(barrier, len(neighbours))
+
+        for device in neighbours:
+
+            @pl.when(device == 0)
+            def _():
+                pl.semaphore_signal(
+                    ready_sem, inc=1, device_id={"seq": device}, device_id_type=MESH
+                )
 
     mine = [
         pltpu.make_async_copy(k_ref.at[:, columns(core, HEAD_DIM)], kraw.at[core], local_sem.at[0]),
@@ -299,7 +316,7 @@
 
     mine[0].wait()
     norm_keys(core)
-    pl.semaphore_wait(barrier, len(greeted))
+    enter()
     swaps[0].start()
     gather_own(kbuf, 0)
     for copy in swaps[1:]:
@@ -524,33 +541,55 @@
 
     lax.fori_loop(0, tile_total, backward, 0)
 
-    def gain_copy(buf, send, recv, place, k, device):
-        return remote(buf.at[place], buf.at[place], send.at[k - 1], recv.at[place], device)
-
-    def gain_start(buf, send, recv, place, total, device_of, value):
-        buf[place] = value
-        for k in range(1, total):
-            gain_copy(buf, send, recv, place, k, device_of(k)).start()
-
-    def gain_finish(buf, send, recv, place, total, device_of):
-        for k in range(1, total):
-            source = lax.rem(place + k, total)
-            gain_copy(buf, send, recv, source, k, device_of(k)).wait_recv()
-        for k in range(1, total):
-            gain_copy(buf, send, recv, place, k, device_of(k)).wait_send()
+    def member_copy(member):
+        return remote(
+            overlap, member_gain.at[member], member_send, member_recv.at[member], 0
+        )
+
+    def cross_copy(place, k):
+        return remote(
+            cross_gain.at[place],
+            cross_gain.at[place],
+            cross_send.at[k],
+            cross_recv.at[place],
+            cross_device(k),
+        )
+
+    def total_copy(member):
+        return remote(total_gain, total_gain, total_send.at[member], total_recv, member)
+
+    def in_order(buf, total):
         value = buf[0]
         for k in range(1, total):
             value = value + buf[k]
         return value
 
-    z_stage = (zgain, zsend, zrecv, 2 * mp + z, chain, z_device)
-    y_stage = (ygain, ysend, yrecv, dp, dp_total, y_device)
-    core_stage = (cgain, csend, crecv, core, 2, lambda k: {"seq": peer})
-    x_stage = (xgain, xsend, xrecv, x, RING, x_device)
-
-    gain_start(*z_stage, overlap[...])
+    def lead_gather():
+        member_gain[0] = overlap[...]
+        for member in range(1, members):
+            member_copy(member).wait_recv()
+        cross_gain[group_place] = in_order(member_gain, members)
+        if group_total > 1:
+            pl.semaphore_wait(barrier, group_total - 1)
+        for k in range(1, group_total):
+            cross_copy(group_place, k).start()
+
+    def lead_spread():
+        for k in range(1, group_total):
+            cross_copy(lax.rem(group_place + k, group_total), k).wait_recv()
+        total_gain[...] = in_order(cross_gain, group_total)
+        for member in range(1, members):
+            total_copy(member).start()
+
+    @pl.when(jnp.logical_not(leader))
+    def _():
+        member_copy(seq).start()
+
     sum_far(*key_refs)
     sum_end(*value_refs)
+
+    pl.when(leader)(lead_gather)
+
     sum_across(*value_refs)
     sum_level(*key_refs)
 
@@ -582,11 +621,6 @@
             sum_beside(*key_refs)
             sum_middle(*key_refs)
             sum_near(*key_refs)
-            gain_start(*y_stage, gain_finish(*z_stage))
-
-        @pl.when(t == 3)
-        def _():
-            gain_start(*core_stage, gain_finish(*y_stage))
 
         return carry
 
@@ -627,8 +661,9 @@
             gvbuf[parity, rows, :] = root_sum(vslot, vland, parity, s).astype(BF16)
     put_out(2)
 
+    pl.when(leader)(lead_spread)
+
     sum_across(*key_refs)
-    gain_start(*x_stage, gain_finish(*core_stage))
     sum_end(*key_refs)
     for number, parity in ((7, 0), (6, 1)):
         sum_copy(ksend, kland, 1, number, parity).wait_recv()
@@ -652,7 +687,19 @@
         if parity is other:
             remotes_out[3].start()
     locals_out[3].start()
-    products = jnp.sum(gain_finish(*x_stage), axis=0, keepdims=True) * scale
+    @pl.when(jnp.logical_not(leader))
+    def _():
+        total_copy(0).wait_recv()
+        member_copy(seq).wait_send()
+
+    @pl.when(leader)
+    def _():
+        for k in range(1, group_total):
+            cross_copy(group_place, k).wait_send()
+        for member in range(1, members):
+            total_copy(member).wait_send()
+
+    products = jnp.sum(total_gain[...], axis=0, keepdims=True) * scale
     gain_out[...] = products / gains_ref[...]
 
     for copy in swaps:
@@ -740,10 +787,9 @@
         pltpu.VMEM(turned, BF16),
         pltpu.VMEM((8, HEAD_DIM), F32),
         pltpu.VMEM((HEAD_DIM, HEAD_DIM), F32),
-        pltpu.VMEM((2 * mp_total, 8, HEAD_DIM), F32),
-        pltpu.VMEM((dp_total, 8, HEAD_DIM), F32),
-        pltpu.VMEM((2, 8, HEAD_DIM), F32),
-        pltpu.VMEM((RING, 8, HEAD_DIM), F32),
+        pltpu.VMEM((4 * RING, 8, HEAD_DIM), F32),
+        pltpu.VMEM((dp_total * mp_total, 8, HEAD_DIM), F32),
+        pltpu.VMEM((8, HEAD_DIM), F32),
         dma((4,)),
         dma((4,)),
         dma((4,)),
@@ -754,14 +800,13 @@
         dma((4,)),
         dma((4,)),
         dma((4,)),
-        dma((2 * mp_total,)),
-        dma((2 * mp_total,)),
-        dma((dp_total,)),
-        dma((dp_total,)),
-        dma((2,)),
-        dma((2,)),
-        dma((RING,)),
-        dma((RING,)),
+        pltpu.SemaphoreType.REGULAR,
+        dma(()),
+        dma((4 * RING,)),
+        dma((dp_total * mp_total,)),
+        dma((dp_total * mp_total,)),
+        dma((4 * RING,)),
+        dma(()),
     ]
     attended, grad_queries, grad_keys, grad_values, grad_gains = pl.pallas_call(
         functools.partial(kernel, images, group, dp_total, mp_total),

time: 81.1 us -> 77.1 us (0.951)
  Pallas kernels: 80.2 us -> 76.2 us
    pallas_call x1, Pallas kernels: 77.5 us -> 73.5 us  [on_device(): pl.pallas_call(functools.partial(kernel, images, group, dp_total, mp_tota...]
where the time goes in v4:
time: 77.1 us; the launch traced here: 76.9 us
  Pallas kernels  76.2 us (99%)
    pallas_call x1, Pallas kernels, on_device(): pl.pallas_call(functools.partial(kernel, images, group, dp_total, mp_tota...  73.5 us
    pallas_call x1, Pallas kernels, on_device(): pl.pallas_call(functools.partial(mover, len(results)), out_shape=[jax.Sha...  2.77 us

profile of v4, /device:TPU:1, one launch (start us, length us, event | category | flops | bytes accessed | tf_op | source)
XLA Modules:
  0.0 76.9 jit_solution(3702112376723714874)
XLA Ops:
  0.6 73.5 %shard_map.110 = (bf16[256,2048]{1,0:T(8,128)(2,1)}, bf16[256,2048]{1,0:T(8,128)(2,1)}, bf16[512,256]{1,0:T(8,128)(2,1)}, bf16[512,256]{1,0:T(8,128)(2,1)}, f32[2,128]{1,0:T(2,128)}) custom-call(bf16[256,2048]{1,0:T(8,128)(2,1)} %bitcast.12, bf16[256,2048]{1,0:T(8,128)(2,1)} %bitcast.13, bf16[512,256]{1,0:T(8,128)(2,1)} %bitcast.14, ...), custom_call_target="tpu_custom_call" | custom-call | tf_op jit(solution)/shard_map/pallas_call | solution.py:811
  74.1 2.8 %shard_map.111 = (bf16[256,2048]{1,0:T(8,128)(2,1)}, bf16[256,2048]{1,0:T(8,128)(2,1)}, bf16[512,256]{1,0:T(8,128)(2,1)}, bf16[512,256]{1,0:T(8,128)(2,1)}, f32[2,128]{1,0:T(2,128)}) custom-call(bf16[256,2048]{1,0:T(8,128)(2,1)} %get-tuple-element.15.refs_0_, bf16[256,2048]{1,0:T(8,128)(2,1)} %get-tuple-element.16.refs_1_, ...), custom_call_target="tpu_custom_call" | custom-call | tf_op jit(solution)/shard_map/pallas_call | solution.py:836

commit v5 on v4

--- a/solution.py
+++ b/solution.py
@@ -66,6 +66,9 @@
     gkbuf,
     gvbuf,
     early,
+    mirror,
+    peer_share,
+    kother,
     unit_keys,
     inverse_keys,
     oturn,
@@ -84,6 +87,7 @@
     out_local,
     out_send,
     out_recv,
+    share_sems,
     ready_sem,
     member_send,
     member_recv,
@@ -181,6 +185,7 @@
         ),
         pltpu.make_async_copy(q_ref.at[:, columns(core, half)], q4.at[own_rows], local_sem.at[2]),
         pltpu.make_async_copy(do_ref.at[:, columns(core, half)], do4.at[own_rows], local_sem.at[3]),
+        pltpu.make_async_copy(k_ref.at[:, columns(other, HEAD_DIM)], kother, local_sem.at[4]),
     ]
     for copy in mine:
         copy.start()
@@ -304,25 +309,29 @@
 
     key_gain = gains_ref[1:2, :]
 
-    def norm_keys(parity):
+    def norm_rows(entries, place, rows):
+        inverse = lax.rsqrt(jnp.mean(entries * entries, axis=-1, keepdims=True) + EPSILON)
+        unit = entries * inverse
+        if place is not None:
+            unit_keys[place, rows, :] = unit
+            inverse_keys[place, rows, :] = inverse
+        return unit
+
+    def norm_keys(parity, place):
         for s in range(subs):
             rows = slice(s * TILE_TOK, (s + 1) * TILE_TOK)
-            entries = kraw[parity, rows, :].astype(F32)
-            inverse = lax.rsqrt(jnp.mean(entries * entries, axis=-1, keepdims=True) + EPSILON)
-            unit = entries * inverse
-            unit_keys[parity, rows, :] = unit
-            inverse_keys[parity, rows, :] = inverse
+            unit = norm_rows(kraw[parity, rows, :].astype(F32), place, rows)
             kbuf[chip + parity, rows, :] = (unit * key_gain).astype(BF16)
 
     mine[0].wait()
-    norm_keys(core)
+    norm_keys(core, core)
     enter()
     swaps[0].start()
     gather_own(kbuf, 0)
     for copy in swaps[1:]:
         copy.start()
     swaps[0].wait_recv()
-    norm_keys(other)
+    norm_keys(other, None)
     gather_swapped(kbuf, 0)
 
     gcol[...] = jnp.transpose(jnp.broadcast_to(gains_ref[0:1, :], (HEAD_DIM, HEAD_DIM)))
@@ -351,14 +360,23 @@
         return carry
 
     lax.fori_loop(0, tile_total, prepare, 0)
+
+    mine[4].wait()
+    for s in range(subs):
+        rows = slice(s * TILE_TOK, (s + 1) * TILE_TOK)
+        norm_rows(kother[rows, :].astype(F32), other, rows)
+
     gather_second(kbuf, 0)
     gather_third(kbuf, 0)
-    gather_fourth(kbuf, 0)
-
     mine[1].wait()
     swaps[1].wait_recv()
-    gather_own(vbuf, 1)
-    gather_swapped(vbuf, 1)
+    gather_across(vbuf, 1, core).start()
+    gather_across(vbuf, 1, other).start()
+    gather_fourth(kbuf, 0)
+    gather_ahead(vbuf, 1, core).start()
+    gather_behind(vbuf, 1, other).start()
+    gather_ahead(vbuf, 1, other).start()
+    gather_behind(vbuf, 1, core).start()
     gather_last(kbuf, 0)
 
     def forward(t, carry):
@@ -427,9 +445,19 @@
     def sum_copy(send, land, which, number, parity):
         image, device = sum_route(number, parity)
         slot = (number - 1) * 2 + parity
+        place = slot
+        if which == 1 and number in (4, 6, 7):
+            place = (number - 1) * 2 + core
+            device = device - core + parity
         return remote(
-            send.at[image], land.at[slot], rs_send.at[which, slot], rs_recv.at[which, slot], device
+            send.at[image], land.at[place], rs_send.at[which, slot], rs_recv.at[which, place], device
         )
+
+    def root_wait(send, land, which, number, head):
+        place = (number - 1) * 2 + head
+        remote(
+            send.at[0], land.at[place], rs_send.at[which, 0], rs_recv.at[which, place], across
+        ).wait_recv()
 
     def share(slot_ref, image, s):
         rows = slice(s * TILE_TOK, (s + 1) * TILE_TOK)
@@ -632,7 +660,6 @@
         (obuf.at[own_rows], obuf.at[other_rows], o_out, out_cols),
         (dqbuf.at[own_rows], dqbuf.at[other_rows], dq_out, out_cols),
         (gvbuf.at[core], gvbuf.at[other], dv_out, head_cols),
-        (gkbuf.at[core], gkbuf.at[other], dk_out, head_cols),
     ]
     locals_out = [
         pltpu.make_async_copy(own, out.at[:, cols], out_local.at[i])
@@ -663,30 +690,49 @@
 
     pl.when(leader)(lead_spread)
 
+    for s in range(subs):
+        rows = slice(s * TILE_TOK, (s + 1) * TILE_TOK)
+        mirror[rows, :] = share(kslot, chip + other, s)
+        early[core, rows, :] = share(kslot, chip + core, s)
+    share_copy = remote(mirror, peer_share, share_sems.at[0], share_sems.at[1], peer)
+    share_copy.start()
     sum_across(*key_refs)
     sum_end(*key_refs)
-    for number, parity in ((7, 0), (6, 1)):
-        sum_copy(ksend, kland, 1, number, parity).wait_recv()
+    share_copy.wait()
+    near, late = 7 - core, 6 + core
+    for head in (0, 1):
+        root_wait(ksend, kland, 1, near, head)
+    for s in range(subs):
+        rows = slice(s * TILE_TOK, (s + 1) * TILE_TOK)
+        place = (near - 1) * 2
+        early[core, rows, :] += kland[place + core, rows, :].astype(F32)
+        early[other, rows, :] = peer_share[rows, :] + kland[place + other, rows, :].astype(F32)
+    for number in (4, late):
+        for head in (0, 1):
+            root_wait(ksend, kland, 1, number, head)
+    sum_last(ksend, kland, 1, ())
+    last_out = []
+    for head in (0, 1):
         for s in range(subs):
             rows = slice(s * TILE_TOK, (s + 1) * TILE_TOK)
-            early[parity, rows, :] = summed(kslot, kland, chip + parity, [(number, parity)], s)
-    sum_last(ksend, kland, 1, ((4, 0), (4, 1), (6, 0), (7, 1)))
-    for parity in (other, core):
-        for s in range(subs):
-            rows = slice(s * TILE_TOK, (s + 1) * TILE_TOK)
-            grads = early[parity, rows, :]
-            for slot in (6 + parity, 10 + 3 * parity):
-                grads = grads + kland[slot, rows, :].astype(F32)
+            grads = early[head, rows, :]
+            for number in (4, late):
+                grads = grads + kland[(number - 1) * 2 + head, rows, :].astype(F32)
             grads = grads * scale
-            unit = unit_keys[parity, rows, :]
+            unit = unit_keys[head, rows, :]
             scaled = grads * key_gain
             mean = jnp.mean(scaled * unit, axis=-1, keepdims=True)
-            gkbuf[parity, rows, :] = (
-                inverse_keys[parity, rows, :] * (scaled - unit * mean)
+            gkbuf[head, rows, :] = (
+                inverse_keys[head, rows, :] * (scaled - unit * mean)
             ).astype(BF16)
-        if parity is other:
-            remotes_out[3].start()
-    locals_out[3].start()
+        last_out.append(
+            pltpu.make_async_copy(
+                gkbuf.at[head],
+                dk_out.at[:, head * HEAD_DIM : (head + 1) * HEAD_DIM],
+                out_local.at[3 + head],
+            )
+        )
+        last_out[head].start()
     @pl.when(jnp.logical_not(leader))
     def _():
         total_copy(0).wait_recv()
@@ -704,6 +750,8 @@
 
     for copy in swaps:
         copy.wait_send()
+    for copy in last_out:
+        copy.wait()
     for i in range(len(results)):
         locals_out[i].wait()
         remotes_out[i].wait_send()
@@ -782,6 +830,9 @@
         pltpu.VMEM((2, max_tokens, HEAD_DIM), BF16),
         pltpu.VMEM((2, max_tokens, HEAD_DIM), BF16),
         pltpu.VMEM((2, max_tokens, HEAD_DIM), F32),
+        pltpu.VMEM((max_tokens, HEAD_DIM), F32),
+        pltpu.VMEM((max_tokens, HEAD_DIM), F32),
+        pltpu.VMEM((max_tokens, HEAD_DIM), BF16),
         pltpu.VMEM((2, max_tokens, HEAD_DIM), F32),
         pltpu.VMEM((2, max_tokens, 1), F32),
         pltpu.VMEM(turned, BF16),
@@ -790,16 +841,17 @@
         pltpu.VMEM((4 * RING, 8, HEAD_DIM), F32),
         pltpu.VMEM((dp_total * mp_total, 8, HEAD_DIM), F32),
         pltpu.VMEM((8, HEAD_DIM), F32),
-        dma((4,)),
-        dma((4,)),
-        dma((4,)),
+        dma((5,)),
+        dma((5,)),
+        dma((5,)),
         dma((2, 14)),
         dma((2, 14)),
         dma((2, 14)),
         dma((2, 14)),
+        dma((5,)),
         dma((4,)),
         dma((4,)),
-        dma((4,)),
+        dma((2,)),
         pltpu.SemaphoreType.REGULAR,
         dma(()),
         dma((4 * RING,)),

time: 77.1 us -> 76.3 us (0.990)
    pallas_call x1, Pallas kernels: 73.5 us -> 72.7 us  [on_device(): pl.pallas_call(functools.partial(kernel, images, group, dp_total, mp_tota...]
where the time goes in v5:
time: 76.3 us; the launch traced here: 76.1 us
  Pallas kernels  75.5 us (99%)
    pallas_call x1, Pallas kernels, on_device(): pl.pallas_call(functools.partial(kernel, images, group, dp_total, mp_tota...  72.7 us
    pallas_call x1, Pallas kernels, on_device(): pl.pallas_call(functools.partial(mover, len(results)), out_shape=[jax.Sha...  2.77 us

profile of v5, /device:TPU:1, one launch (start us, length us, event | category | flops | bytes accessed | tf_op | source)
XLA Modules:
  0.0 76.1 jit_solution(9610521411171141352)
XLA Ops:
  0.6 72.7 %shard_map.110 = (bf16[256,2048]{1,0:T(8,128)(2,1)}, bf16[256,2048]{1,0:T(8,128)(2,1)}, bf16[512,256]{1,0:T(8,128)(2,1)}, bf16[512,256]{1,0:T(8,128)(2,1)}, f32[2,128]{1,0:T(2,128)}) custom-call(bf16[256,2048]{1,0:T(8,128)(2,1)} %bitcast.12, bf16[256,2048]{1,0:T(8,128)(2,1)} %bitcast.13, bf16[512,256]{1,0:T(8,128)(2,1)} %bitcast.14, ...), custom_call_target="tpu_custom_call" | custom-call | tf_op jit(solution)/shard_map/pallas_call | solution.py:863
  73.3 2.8 %shard_map.111 = (bf16[256,2048]{1,0:T(8,128)(2,1)}, bf16[256,2048]{1,0:T(8,128)(2,1)}, bf16[512,256]{1,0:T(8,128)(2,1)}, bf16[512,256]{1,0:T(8,128)(2,1)}, f32[2,128]{1,0:T(2,128)}) custom-call(bf16[256,2048]{1,0:T(8,128)(2,1)} %get-tuple-element.15.refs_0_, bf16[256,2048]{1,0:T(8,128)(2,1)} %get-tuple-element.16.refs_1_, ...), custom_call_target="tpu_custom_call" | custom-call | tf_op jit(solution)/shard_map/pallas_call | solution.py:888

commit v6 on v5

--- a/solution.py
+++ b/solution.py
@@ -15,7 +15,7 @@
 LOG2E = 1.4426950408889634
 MESH = pl.DeviceIdType.MESH
 BF16 = jnp.bfloat16
-MOVE_CUTS = 4
+MOVE_CUTS = 2
 F32 = jnp.float32
 
 RING = 4
@@ -619,6 +619,7 @@
     pl.when(leader)(lead_gather)
 
     sum_across(*value_refs)
+    sum_middle(*key_refs)
     sum_level(*key_refs)
 
     def queries_backward(t, carry):
@@ -647,7 +648,6 @@
         @pl.when(t == 1)
         def _():
             sum_beside(*key_refs)
-            sum_middle(*key_refs)
             sum_near(*key_refs)
 
         return carry

time: 76.3 us -> 75.8 us (level)
  no operation moved by 1% of the time
where the time goes in v6:
time: 75.8 us; the launch traced here: 75.6 us
  Pallas kernels  75 us (99%)
    pallas_call x1, Pallas kernels, on_device(): pl.pallas_call(functools.partial(kernel, images, group, dp_total, mp_tota...  72.3 us
    pallas_call x1, Pallas kernels, on_device(): pl.pallas_call(functools.partial(mover, len(results)), out_shape=[jax.Sha...  2.69 us

profile of v6, /device:TPU:1, one launch (start us, length us, event | category | flops | bytes accessed | tf_op | source)
XLA Modules:
  0.0 75.6 jit_solution(4247025332421674219)
XLA Ops:
  0.6 72.3 %shard_map.110 = (bf16[256,2048]{1,0:T(8,128)(2,1)}, bf16[256,2048]{1,0:T(8,128)(2,1)}, bf16[512,256]{1,0:T(8,128)(2,1)}, bf16[512,256]{1,0:T(8,128)(2,1)}, f32[2,128]{1,0:T(2,128)}) custom-call(bf16[256,2048]{1,0:T(8,128)(2,1)} %bitcast.12, bf16[256,2048]{1,0:T(8,128)(2,1)} %bitcast.13, bf16[512,256]{1,0:T(8,128)(2,1)} %bitcast.14, ...), custom_call_target="tpu_custom_call" | custom-call | tf_op jit(solution)/shard_map/pallas_call | solution.py:863
  72.9 2.7 %shard_map.111 = (bf16[256,2048]{1,0:T(8,128)(2,1)}, bf16[256,2048]{1,0:T(8,128)(2,1)}, bf16[512,256]{1,0:T(8,128)(2,1)}, bf16[512,256]{1,0:T(8,128)(2,1)}, f32[2,128]{1,0:T(2,128)}) custom-call(bf16[256,2048]{1,0:T(8,128)(2,1)} %get-tuple-element.15.refs_0_, bf16[256,2048]{1,0:T(8,128)(2,1)} %get-tuple-element.16.refs_1_, ...), custom_call_target="tpu_custom_call" | custom-call | tf_op jit(solution)/shard_map/pallas_call | solution.py:888
